TPU v7x, 32 devices: a whole 2x2x4 slice. The times are simulated.
32 devices in a mesh: dc: 16 (over z, y, x), kv: 2 (over core).
Axes of the slice: x: 2, y: 2, z: 4, core: 2. Of those that a mesh axis runs over, the one named last changes fastest.
Arguments:
- queries: bfloat16 [5120, 5120], P('dc', 'kv'), may hold values from -41 to 41
- keys: bfloat16 [5120, 1024], P('dc', 'kv'), may hold values from -4 to 4
- values: bfloat16 [5120, 1024], P('dc', 'kv'), may hold values from -6 to 6
- output_gradient: bfloat16 [5120, 5120], P('dc', 'kv'), may hold values from -6 to 6
- segment_ids: int32 [5120], P('dc'), may hold values from 0 to 7, as said below
- w_query: bfloat16 [5120, 5120], P(None, 'kv'), may hold values from -0.078125 to 0.078125
- key_weight_matrix: bfloat16 [5120, 1024], P(None, 'kv'), may hold values from -0.078125 to 0.078125
- value_weight_matrix: bfloat16 [5120, 1024], P(None, 'kv'), may hold values from -0.078125 to 0.078125
Outputs:
- query_grad: bfloat16 [5120, 5120], P('dc', 'kv')
- key_grad: bfloat16 [5120, 1024], P('dc', 'kv')
- value_grad: bfloat16 [5120, 1024], P('dc', 'kv')
- input_grad: bfloat16 [5120, 5120], P('dc', 'kv')
Inputs may be any that keep to these rules, and one draw needn't show every extreme that they name: `segment_ids`: segment ids never fall along the tokens; every document has 1 to 2241 tokens and one has exactly 2241.
All inputs are finite; a program needn't handle non-finite values.
Results may differ from a plain program's by a relative error of at most 0.0065.
Values may be sent and summed in bfloat16 or wider, within the bound.
A program may use at most 448 MiB of HBM per device.

v0:
```python
import jax
import jax.numpy as jnp
from jax import lax
from jax.sharding import PartitionSpec as P

QUERY_HEAD_COUNT = 40
KEY_VALUE_HEADS = 8
HEAD_SIZE = 128
REACH = 8


def entering(value, axis, combine, identity):
    devices, position = (lax.axis_size(axis), lax.axis_index(axis))
    everything = jax.tree.map(lambda part: lax.all_gather(part, axis), value)
    start = jax.tree.map(
        lambda part, zero: jnp.broadcast_to(jnp.asarray(zero, part.dtype), part.shape),
        value,
        identity,
    )

    def step(k, before):
        reached = k < position
        new = combine(before, jax.tree.map(lambda part: part[k], everything))
        return jax.tree.map(lambda a, b: jnp.where(reached, a, b), new, before)

    return lax.fori_loop(0, devices, step, start)


def from_behind(block, axis, distance):
    devices = range(lax.axis_size(axis))
    route = [(i - distance, i) for i in devices if i - distance in devices]
    return lax.ppermute(block, axis, route)


def link_docs(earlier, later):
    keep = (later[2] == 1) & ((later[0] == earlier[0]) | (later[0] < 0))
    whole_flag = jnp.where(keep, earlier[2], later[2] * (earlier[0] < 0).astype(jnp.int32))
    return (
        jnp.where(keep, earlier[0], later[0]),
        jnp.where(keep, earlier[1], later[1]),
        whole_flag,
    )


def shards(
    queries,
    keys,
    values,
    output_gradient,
    segment_ids,
    w_query,
    key_weight_matrix,
    value_weight_matrix,
):
    tok_rows = queries.shape[0]
    group_width = QUERY_HEAD_COUNT // KEY_VALUE_HEADS
    kv_local = keys.shape[1] // HEAD_SIZE
    softmax_scale = HEAD_SIZE ** (-0.5)
    device_pos = lax.axis_index("dc")
    local_pos = jnp.arange(tok_rows, dtype=jnp.int32)
    fresh = jnp.concatenate([jnp.zeros((1,), jnp.bool_), segment_ids[1:] != segment_ids[:-1]])
    latest = lax.cummax(jnp.where(fresh, local_pos, -1), axis=0)
    last_mark = latest[-1:]
    summary = (
        segment_ids[-1:],
        device_pos * tok_rows + jnp.maximum(last_mark, 0),
        (last_mark < 0).astype(jnp.int32),
    )
    identity = (
        jnp.full((1,), -1, jnp.int32),
        jnp.zeros((1,), jnp.int32),
        jnp.ones((1,), jnp.int32),
    )
    before = entering(summary, "dc", link_docs, identity)
    carried = jnp.where(before[0] == segment_ids[:1], before[1], device_pos * tok_rows)
    start_query = jnp.where(latest >= 0, device_pos * tok_rows + latest, carried)
    key_list = [keys]
    value_list = [values]
    for distance in range(1, REACH):
        got_keys, got_values = from_behind((keys, values), "dc", distance)
        key_list.insert(0, got_keys)
        value_list.insert(0, got_values)
    key_window = jnp.concatenate(key_list, axis=0)
    value_window = jnp.concatenate(value_list, axis=0)
    attention_span = REACH * tok_rows
    pos_query = device_pos * tok_rows + local_pos
    pos_key = (device_pos - REACH + 1) * tok_rows + jnp.arange(attention_span, dtype=jnp.int32)
    allowed = (pos_key[None, :] >= start_query[:, None]) & (pos_key[None, :] <= pos_query[:, None])
    query_heads = queries.reshape(tok_rows, kv_local, group_width, HEAD_SIZE)
    grad_heads = output_gradient.reshape(tok_rows, kv_local, group_width, HEAD_SIZE)
    key_heads = key_window.reshape(attention_span, kv_local, HEAD_SIZE)
    value_heads = value_window.reshape(attention_span, kv_local, HEAD_SIZE)
    scores = (
        jnp.einsum("tkgd,skd->kgts", query_heads, key_heads, preferred_element_type=jnp.float32)
        * softmax_scale
    )
    top = jnp.max(jnp.where(allowed, scores, -jnp.inf), axis=-1, keepdims=True)
    expo = jnp.where(allowed, jnp.exp(scores - top), 0.0)
    probs = expo / jnp.sum(expo, axis=-1, keepdims=True)
    probability_narrow = probs.astype(jnp.bfloat16)
    dprobs = jnp.einsum(
        "tkgd,skd->kgts", grad_heads, value_heads, preferred_element_type=jnp.float32
    )
    delta = jnp.sum(probs * dprobs, axis=-1, keepdims=True)
    score_gradient = (probs * (dprobs - delta)).astype(jnp.bfloat16)
    query_grad = (
        (
            jnp.einsum(
                "kgts,skd->tkgd", score_gradient, key_heads, preferred_element_type=jnp.float32
            )
            * softmax_scale
        )
        .astype(jnp.bfloat16)
        .reshape(tok_rows, -1)
    )
    key_terms = (
        jnp.einsum(
            "qwuh,uqwb->hqb", score_gradient, query_heads, preferred_element_type=jnp.float32
        )
        * softmax_scale
    )
    value_terms = jnp.einsum(
        "qwuh,uqwb->hqb", probability_narrow, grad_heads, preferred_element_type=jnp.float32
    )
    key_blocks = key_terms.reshape(REACH, tok_rows, kv_local * HEAD_SIZE)
    value_blocks = value_terms.reshape(REACH, tok_rows, kv_local * HEAD_SIZE)
    key_total = key_blocks[REACH - 1]
    value_total = value_blocks[REACH - 1]
    for distance in range(1, REACH):
        got_keys, got_values = from_behind(
            (key_blocks[REACH - 1 - distance], value_blocks[REACH - 1 - distance]), "dc", -distance
        )
        key_total = key_total + got_keys
        value_total = value_total + got_values
    key_grad = key_total.astype(jnp.bfloat16)
    value_grad = value_total.astype(jnp.bfloat16)
    contract = (((1,), (1,)), ((), ()))
    partial_input = lax.dot_general(
        query_grad, w_query, contract, preferred_element_type=jnp.float32
    )
    partial_input = partial_input + lax.dot_general(
        key_grad, key_weight_matrix, contract, preferred_element_type=jnp.float32
    )
    partial_input = partial_input + lax.dot_general(
        value_grad, value_weight_matrix, contract, preferred_element_type=jnp.float32
    )
    input_grad = lax.psum_scatter(
        partial_input.astype(jnp.bfloat16), "kv", scatter_dimension=1, tiled=True
    )
    return (query_grad, key_grad, value_grad, input_grad)


def solution(mesh):
    in_specs = (
        P("dc", "kv"),
        P("dc", "kv"),
        P("dc", "kv"),
        P("dc", "kv"),
        P("dc"),
        P(None, "kv"),
        P(None, "kv"),
        P(None, "kv"),
    )
    out_specs = (P("dc", "kv"), P("dc", "kv"), P("dc", "kv"), P("dc", "kv"))
    return jax.shard_map(shards, mesh=mesh, in_specs=in_specs, out_specs=out_specs, check_vma=False)
```

profile of v0, /device:TPU:25, one launch (start us, length us, event | category | flops | bytes accessed | tf_op | source)
XLA Modules:
  0.0 728.2 jit_solution(7262573711414867869)
XLA Ops:
  11.5 3.1 collective-permute-start.5
  25.6 14.0 %all-reduce.4 = (s32[16]{0:T(128)S(1)}, s32[16]{0:T(128)S(1)}, s32[16]{0:T(128)S(1)}) all-reduce(s32[16]{0:T(128)S(1)} %fusion.35, s32[16]{0:T(128)S(1)} %get-tuple-element.171, s32[16]{0:T(128)S(1)} %add_dynamic-update-slice_fusion), channel_id=2, replica_groups=mesh['dc'=16,'kv'=2] {'dc'}, use_global_device_ids=true, to_apply=%add.1 | all-reduce | flops 48 | bytes 384
  39.5 72.1 %while.15 = (s32[]{:T(128)}, s32[1]{0:T(128)}, s32[1]{0:T(128)}, s32[]{:T(128)}, s32[16,1]{0,1:T(1,128)S(1)}, /*index=5*/s32[16,1]{0,1:T(1,128)S(1)}, s32[16,1]{0,1:T(1,128)S(1)}, s32[]{:T(128)}, s32[1]{0:T(128)}) while((s32[]{:T(128)}, s32[1]{0:T(128)}, s32[1]{0:T(128)}, s32[]{:T(128)}, s32[16,1]{0,1:T(1,128)S(1)}, ...), condition=%wide.region_3.4_spmd, body=%wide.region_2.3_spmd.sunk | while | flops 12 | bytes 215 | solution.py:26
  117.8 3.6 copy.24
  121.4 4.2 copy.35
  125.6 7.8 %collective-permute-start.13 = (bf16[320,512]{0,1:T(8,128)(2,1)S(1)}, bf16[320,512]{0,1:T(8,128)(2,1)}, u32[]{:S(2)}, u32[]{:S(2)}) collective-permute-start(bf16[320,512]{0,1:T(8,128)(2,1)S(1)} %copy.27), channel_id=1, source_target_pairs={{0,2},{2,4},{4,6},{6,8},{8,10},{10,12},{12,14},{14,16},{16,18},{18... | collective-permute-start | bytes 983048 | tf_op jit(solution)/shard_map/ppermute | solution.py:32
  133.5 24.0 %collective-permute-start.12 = (bf16[320,512]{0,1:T(8,128)(2,1)S(1)}, bf16[320,512]{0,1:T(8,128)(2,1)}, u32[]{:S(2)}, u32[]{:S(2)}) collective-permute-start(bf16[320,512]{0,1:T(8,128)(2,1)S(1)} %copy.27), channel_id=1, source_target_pairs={{0,4},{2,6},{4,8},{6,10},{8,12},{10,14},{12,16},{14,18},{16,20},{1... | collective-permute-start | bytes 983048 | tf_op jit(solution)/shard_map/ppermute | solution.py:32
  162.0 5.5 concatenate.9
  167.5 41.9 %fusion.40 = (f32[4,5,320]{2,1,0:T(8,128)S(1)}, f32[4,5,320,2560]{3,2,1,0:T(8,128)}) fusion(pred[320,2560]{1,0:T(8,128)(4,1)} %compare_and_fusion, bf16[2560,4,128,1]{0,2,3,1:T(8,128)(2,1)} %bitcast.204, bf16[320,4,5,128]{0,3,2,1:T(8,128)(2,1)S(1)} %bitcast.198), kind=kOutput, calls=%fused_computation.93 | convolution fusion | flops 8486914048 | bytes 70640640 | tf_op jit(solution)/shard_map/sub | solution.py:98
  212.1 27.3 %fusion.17 = f32[2560,4,128]{2,0,1:T(8,128)} fusion(bf16[320,4,5,128]{0,3,2,1:T(8,128)(2,1)} %bitcast.207, f32[4,5,320,2560]{3,2,1,0:T(8,128)} %get-tuple-element.173, f32[4,5,320]{2,1,0:T(8,128)S(1)} %get-tuple-element.172), kind=kOutput, calls=%fused_computation.27 | convolution fusion | flops 4227072000 | bytes 72442880 | tf_op jit(solution)/shard_map/qwuh,uqwb->hqb/dot_general | solution.py:122
  239.5 3.3 collective-permute-done.9
  243.4 4.3 concatenate.11
  247.7 47.4 %fusion.1 = (f32[4,5,320]{2,1,0:T(8,128)S(1)}, f32[4,2560,320,5]{1,2,3,0:T(8,128)}) fusion(f32[4,5,320,2560]{3,2,1,0:T(8,128)} %get-tuple-element.173, f32[4,5,320]{2,1,0:T(8,128)S(1)} %get-tuple-element.172, bf16[2560,4,128,1]{0,2,3,1:T(8,128)(2,1)S(1)} %bitcast.206, bf16[320,4,5,128]{0,3,2,1:T(8,128)(2,1)} %bitcast.208), kind=kOutput, calls=%fused_computation.6 | convolution fusion | flops 4243449600 | bytes 135383040 | tf_op jit(solution)/shard_map/tkgd,skd->kgts/dot_general | solution.py:101
  295.1 51.8 %fusion.3 = bf16[4,5,320,2560]{3,2,1,0:T(8,128)(2,1)} fusion(f32[4,2560,320,5]{1,2,3,0:T(8,128)} %get-tuple-element.175, f32[4,5,320]{2,1,0:T(8,128)S(1)} %get-tuple-element.174, f32[4,5,320,2560]{3,2,1,0:T(8,128)} %get-tuple-element.173, f32[4,5,320]{2,1,0:T(8,128)S(1)} %get-tuple-element.172), kind=kLoop, calls=%fused_computation.8 | loop fusion | flops 65536000 | bytes 163891200 | tf_op jit(solution)/shard_map/convert_element_type | solution.py:105
  346.8 19.6 %fusion.16 = f32[2560,4,128]{2,0,1:T(8,128)} fusion(bf16[4,5,320,2560]{3,2,1,0:T(8,128)(2,1)} %fusion.3, bf16[320,4,5,128]{0,3,2,1:T(8,128)(2,1)S(1)} %bitcast.199), kind=kOutput, calls=%fused_computation.26 | convolution fusion | flops 4195614720 | bytes 39649280 | tf_op jit(solution)/shard_map/qwuh,uqwb->hqb/dot_general | solution.py:117
  366.4 4.3 slice_bitcast_fusion.15
  377.3 8.3 %collective-permute-start.15 = (f32[320,512]{1,0:T(8,128)}, f32[320,512]{1,0:T(8,128)}, u32[]{:S(2)}, u32[]{:S(2)}) collective-permute-start(f32[320,512]{1,0:T(8,128)} %bitcast.186), channel_id=1, source_target_pairs={{4,0},{6,2},{8,4},{10,6},{12,8},{14,10},{16,12},{18,14},{20,16},{2... | collective-permute-start | bytes 1966088 | tf_op jit(solution)/shard_map/ppermute | solution.py:32
  385.6 15.0 %collective-permute-start.16 = (f32[320,512]{1,0:T(8,128)}, f32[320,512]{1,0:T(8,128)}, u32[]{:S(2)}, u32[]{:S(2)}) collective-permute-start(f32[320,512]{1,0:T(8,128)} %bitcast.185), channel_id=1, source_target_pairs={{6,0},{8,2},{10,4},{12,6},{14,8},{16,10},{18,12},{20,14},{22,16},{... | collective-permute-start | bytes 1966088 | tf_op jit(solution)/shard_map/ppermute | solution.py:32
  400.6 3.2 collective-permute-start.17
  403.8 15.4 %fusion.20 = bf16[320,4,5,128]{3,0,2,1:T(8,128)(2,1)} fusion(bf16[2560,4,128,1]{0,2,3,1:T(8,128)(2,1)S(1)} %bitcast.205, bf16[4,5,320,2560]{3,2,1,0:T(8,128)(2,1)} %fusion.3), kind=kOutput, calls=%fused_computation.30 | convolution fusion | flops 4195942400 | bytes 37027840 | tf_op jit(solution)/shard_map/kgts,skd->tkgd/dot_general | solution.py:108
  438.7 13.7 %collective-permute-start.19 = (f32[320,512]{1,0:T(8,128)}, f32[320,512]{1,0:T(8,128)}, u32[]{:S(2)}, u32[]{:S(2)}) collective-permute-start(f32[320,512]{1,0:T(8,128)} %bitcast.182), channel_id=1, source_target_pairs={{12,0},{14,2},{16,4},{18,6},{20,8},{22,10},{24,12},{26,14},{28,16}... | collective-permute-start | bytes 1966088 | tf_op jit(solution)/shard_map/ppermute | solution.py:32
  452.4 13.1 %collective-permute-start.20 = (f32[320,512]{1,0:T(8,128)}, f32[320,512]{1,0:T(8,128)}, u32[]{:S(2)}, u32[]{:S(2)}) collective-permute-start(f32[320,512]{1,0:T(8,128)} %bitcast.181), channel_id=1, source_target_pairs={{14,0},{16,2},{18,4},{20,6},{22,8},{24,10},{26,12},{28,14},{30,16}... | collective-permute-start | bytes 1966088 | tf_op jit(solution)/shard_map/ppermute | solution.py:32
  465.6 18.7 %fusion.41 = f32[320,5120]{1,0:T(8,128)} fusion(bf16[320,2560]{0,1:T(8,128)(2,1)S(1)} %bitcast.196, bf16[5120,2560]{1,0:T(8,128)(2,1)} %param.15), kind=kOutput, calls=%fused_computation.94 | convolution fusion | flops 8388608000 | bytes 34406400 | tf_op jit(solution)/shard_map/dot_general | solution.py:138
  488.5 46.1 %collective-permute-start.23 = (f32[320,512]{1,0:T(8,128)S(1)}, f32[320,512]{1,0:T(8,128)S(1)}, u32[]{:S(2)}, u32[]{:S(2)}) collective-permute-start(f32[320,512]{1,0:T(8,128)S(1)} %bitcast.214), channel_id=1, source_target_pairs={{6,0},{8,2},{10,4},{12,6},{14,8},{16,10},{18,12},{20,14},{22,16},{... | collective-permute-start | bytes 1966088 | tf_op jit(solution)/shard_map/ppermute | solution.py:32
  534.6 43.3 %collective-permute-start.24 = (f32[320,512]{1,0:T(8,128)S(1)}, f32[320,512]{1,0:T(8,128)S(1)}, u32[]{:S(2)}, u32[]{:S(2)}) collective-permute-start(f32[320,512]{1,0:T(8,128)S(1)} %bitcast.213), channel_id=1, source_target_pairs={{8,0},{10,2},{12,4},{14,6},{16,8},{18,10},{20,12},{22,14},{24,16},... | collective-permute-start | bytes 1966088 | tf_op jit(solution)/shard_map/ppermute | solution.py:32
  582.9 19.5 %collective-permute-start.26 = (f32[320,512]{1,0:T(8,128)S(1)}, f32[320,512]{1,0:T(8,128)}, u32[]{:S(2)}, u32[]{:S(2)}) collective-permute-start(f32[320,512]{1,0:T(8,128)S(1)} %bitcast.211), channel_id=1, source_target_pairs={{12,0},{14,2},{16,4},{18,6},{20,8},{22,10},{24,12},{26,14},{28,16}... | collective-permute-start | bytes 1966088 | tf_op jit(solution)/shard_map/ppermute | solution.py:32
  604.8 4.5 convolution_add_fusion.1
  609.4 8.4 %collective-permute-done.26 = f32[320,512]{1,0:T(8,128)} collective-permute-done((f32[320,512]{1,0:T(8,128)S(1)}, f32[320,512]{1,0:T(8,128)}, u32[]{:S(2)}, u32[]{:S(2)}) %collective-permute-start.26) | collective-permute-done | bytes 655392 | tf_op jit(solution)/shard_map/ppermute | solution.py:32
  617.7 14.0 %collective-permute-done.27 = f32[320,512]{1,0:T(8,128)} collective-permute-done((f32[320,512]{1,0:T(8,128)S(1)}, f32[320,512]{1,0:T(8,128)}, u32[]{:S(2)}, u32[]{:S(2)}) %collective-permute-start.27) | collective-permute-done | bytes 655392 | tf_op jit(solution)/shard_map/ppermute | solution.py:32
  634.2 3.7 fusion.13
  637.9 3.3 copy.58
  641.2 79.8 %reduce-scatter.2.cloned.1.call-done = bf16[320,2560]{1,0:T(8,128)(2,1)} async-done(((bf16[320,5120]{1,0:T(8,128)(2,1)}), bf16[320,2560]{1,0:T(8,128)(2,1)}) %reduce-scatter.2.cloned.1.call-update) | async-done | bytes 1638416 | tf_op jit(solution)/shard_map/reduce_scatter | solution.py:147
  (143 shorter events, 89.3 us)
Async XLA Ops:
  7.2 713.8 %reduce-scatter.2.cloned.1.call-start = ((), (), s32[]{:S(2)}) async-start(), calls=%async_computation.1 | async-start | bytes 4915200 | tf_op jit(solution)/shard_map/reduce_scatter | solution.py:147
  8.4 103.9 %collective-permute-start.6 = (bf16[320,512]{0,1:T(8,128)(2,1)S(1)}, bf16[320,512]{0,1:T(8,128)(2,1)S(1)}, u32[]{:S(2)}, u32[]{:S(2)}) collective-permute-start(bf16[320,512]{0,1:T(8,128)(2,1)S(1)} %copy.16), channel_id=1, source_target_pairs={{0,2},{2,4},{4,6},{6,8},{8,10},{10,12},{12,14},{14,16},{16,18},{18... | collective-permute-start | bytes 983048 | tf_op jit(solution)/shard_map/ppermute | solution.py:32
  11.5 102.1 %collective-permute-start.5 = (bf16[320,512]{0,1:T(8,128)(2,1)S(1)}, bf16[320,512]{0,1:T(8,128)(2,1)S(1)}, u32[]{:S(2)}, u32[]{:S(2)}) collective-permute-start(bf16[320,512]{0,1:T(8,128)(2,1)S(1)} %copy.16), channel_id=1, source_target_pairs={{0,4},{2,6},{4,8},{6,10},{8,12},{10,14},{12,16},{14,18},{16,20},{1... | collective-permute-start | bytes 983048 | tf_op jit(solution)/shard_map/ppermute | solution.py:32
  14.7 110.9 %collective-permute-start.4 = (bf16[320,512]{0,1:T(8,128)(2,1)S(1)}, bf16[320,512]{0,1:T(8,128)(2,1)}, u32[]{:S(2)}, u32[]{:S(2)}) collective-permute-start(bf16[320,512]{0,1:T(8,128)(2,1)S(1)} %copy.16), channel_id=1, source_target_pairs={{0,6},{2,8},{4,10},{6,12},{8,14},{10,16},{12,18},{14,20},{16,22},{... | collective-permute-start | bytes 983048 | tf_op jit(solution)/shard_map/ppermute | solution.py:32
  16.6 116.8 %collective-permute-start.3 = (bf16[320,512]{0,1:T(8,128)(2,1)S(1)}, bf16[320,512]{0,1:T(8,128)(2,1)}, u32[]{:S(2)}, u32[]{:S(2)}) collective-permute-start(bf16[320,512]{0,1:T(8,128)(2,1)S(1)} %copy.16), channel_id=1, source_target_pairs={{0,8},{2,10},{4,12},{6,14},{8,16},{10,18},{12,20},{14,22},{16,24},... | collective-permute-start | bytes 983048 | tf_op jit(solution)/shard_map/ppermute | solution.py:32
  17.9 139.5 %collective-permute-start.2 = (bf16[320,512]{0,1:T(8,128)(2,1)S(1)}, bf16[320,512]{0,1:T(8,128)(2,1)}, u32[]{:S(2)}, u32[]{:S(2)}) collective-permute-start(bf16[320,512]{0,1:T(8,128)(2,1)S(1)} %copy.16), channel_id=1, source_target_pairs={{0,10},{2,12},{4,14},{6,16},{8,18},{10,20},{12,22},{14,24},{16,26}... | collective-permute-start | bytes 983048 | tf_op jit(solution)/shard_map/ppermute | solution.py:32
  112.3 47.1 %collective-permute-start.1 = (bf16[320,512]{0,1:T(8,128)(2,1)S(1)}, bf16[320,512]{0,1:T(8,128)(2,1)}, u32[]{:S(2)}, u32[]{:S(2)}) collective-permute-start(bf16[320,512]{0,1:T(8,128)(2,1)S(1)} %copy.16), channel_id=1, source_target_pairs={{0,12},{2,14},{4,16},{6,18},{8,20},{10,22},{12,24},{14,26},{16,28}... | collective-permute-start | bytes 983048 | tf_op jit(solution)/shard_map/ppermute | solution.py:32
  113.6 47.1 %collective-permute-start = (bf16[320,512]{0,1:T(8,128)(2,1)S(1)}, bf16[320,512]{0,1:T(8,128)(2,1)}, u32[]{:S(2)}, u32[]{:S(2)}) collective-permute-start(bf16[320,512]{0,1:T(8,128)(2,1)S(1)} %copy.16), channel_id=1, source_target_pairs={{0,14},{2,16},{4,18},{6,20},{8,22},{10,24},{12,26},{14,28},{16,30}... | collective-permute-start | bytes 983048 | tf_op jit(solution)/shard_map/ppermute | solution.py:32
  121.4 88.0 %copy-start.1 = (bf16[320,2560]{0,1:T(8,128)(2,1)}, bf16[320,2560]{0,1:T(8,128)(2,1)S(1)}, u32[]{:S(2)}) copy-start(bf16[320,2560]{0,1:T(8,128)(2,1)S(1)} %copy.24) | copy-start | bytes 4915204
  125.6 83.7 %collective-permute-start.13 = (bf16[320,512]{0,1:T(8,128)(2,1)S(1)}, bf16[320,512]{0,1:T(8,128)(2,1)}, u32[]{:S(2)}, u32[]{:S(2)}) collective-permute-start(bf16[320,512]{0,1:T(8,128)(2,1)S(1)} %copy.27), channel_id=1, source_target_pairs={{0,2},{2,4},{4,6},{6,8},{8,10},{10,12},{12,14},{14,16},{16,18},{18... | collective-permute-start | bytes 983048 | tf_op jit(solution)/shard_map/ppermute | solution.py:32
  133.5 77.2 %collective-permute-start.12 = (bf16[320,512]{0,1:T(8,128)(2,1)S(1)}, bf16[320,512]{0,1:T(8,128)(2,1)}, u32[]{:S(2)}, u32[]{:S(2)}) collective-permute-start(bf16[320,512]{0,1:T(8,128)(2,1)S(1)} %copy.27), channel_id=1, source_target_pairs={{0,4},{2,6},{4,8},{6,10},{8,12},{10,14},{12,16},{14,18},{16,20},{1... | collective-permute-start | bytes 983048 | tf_op jit(solution)/shard_map/ppermute | solution.py:32
  157.4 82.0 %collective-permute-start.11 = (bf16[320,512]{0,1:T(8,128)(2,1)S(1)}, bf16[320,512]{0,1:T(8,128)(2,1)}, u32[]{:S(2)}, u32[]{:S(2)}) collective-permute-start(bf16[320,512]{0,1:T(8,128)(2,1)S(1)} %copy.27), channel_id=1, source_target_pairs={{0,6},{2,8},{4,10},{6,12},{8,14},{10,16},{12,18},{14,20},{16,22},{... | collective-permute-start | bytes 983048 | tf_op jit(solution)/shard_map/ppermute | solution.py:32
  159.4 80.1 %collective-permute-start.10 = (bf16[320,512]{0,1:T(8,128)(2,1)S(1)}, bf16[320,512]{0,1:T(8,128)(2,1)}, u32[]{:S(2)}, u32[]{:S(2)}) collective-permute-start(bf16[320,512]{0,1:T(8,128)(2,1)S(1)} %copy.27), channel_id=1, source_target_pairs={{0,8},{2,10},{4,12},{6,14},{8,16},{10,18},{12,20},{14,22},{16,24},... | collective-permute-start | bytes 983048 | tf_op jit(solution)/shard_map/ppermute | solution.py:32
  160.7 82.1 %collective-permute-start.9 = (bf16[320,512]{0,1:T(8,128)(2,1)S(1)}, bf16[320,512]{0,1:T(8,128)(2,1)}, u32[]{:S(2)}, u32[]{:S(2)}) collective-permute-start(bf16[320,512]{0,1:T(8,128)(2,1)S(1)} %copy.27), channel_id=1, source_target_pairs={{0,10},{2,12},{4,14},{6,16},{8,18},{10,20},{12,22},{14,24},{16,26}... | collective-permute-start | bytes 983048 | tf_op jit(solution)/shard_map/ppermute | solution.py:32
  209.4 34.0 %collective-permute-start.8 = (bf16[320,512]{0,1:T(8,128)(2,1)S(1)}, bf16[320,512]{0,1:T(8,128)(2,1)S(1)}, u32[]{:S(2)}, u32[]{:S(2)}) collective-permute-start(bf16[320,512]{0,1:T(8,128)(2,1)S(1)} %copy.27), channel_id=1, source_target_pairs={{0,12},{2,14},{4,16},{6,18},{8,20},{10,22},{12,24},{14,26},{16,28}... | collective-permute-start | bytes 983048 | tf_op jit(solution)/shard_map/ppermute | solution.py:32
  210.7 32.7 %collective-permute-start.7 = (bf16[320,512]{0,1:T(8,128)(2,1)S(1)}, bf16[320,512]{0,1:T(8,128)(2,1)}, u32[]{:S(2)}, u32[]{:S(2)}) collective-permute-start(bf16[320,512]{0,1:T(8,128)(2,1)S(1)} %copy.27), channel_id=1, source_target_pairs={{0,14},{2,16},{4,18},{6,20},{8,22},{10,24},{12,26},{14,28},{16,30}... | collective-permute-start | bytes 983048 | tf_op jit(solution)/shard_map/ppermute | solution.py:32
  374.5 60.2 %collective-permute-start.14 = (f32[320,512]{1,0:T(8,128)}, f32[320,512]{1,0:T(8,128)}, u32[]{:S(2)}, u32[]{:S(2)}) collective-permute-start(f32[320,512]{1,0:T(8,128)} %bitcast.187), channel_id=1, source_target_pairs={{2,0},{4,2},{6,4},{8,6},{10,8},{12,10},{14,12},{16,14},{18,16},{20... | collective-permute-start | bytes 1966088 | tf_op jit(solution)/shard_map/ppermute | solution.py:32
  377.3 59.3 %collective-permute-start.15 = (f32[320,512]{1,0:T(8,128)}, f32[320,512]{1,0:T(8,128)}, u32[]{:S(2)}, u32[]{:S(2)}) collective-permute-start(f32[320,512]{1,0:T(8,128)} %bitcast.186), channel_id=1, source_target_pairs={{4,0},{6,2},{8,4},{10,6},{12,8},{14,10},{16,12},{18,14},{20,16},{2... | collective-permute-start | bytes 1966088 | tf_op jit(solution)/shard_map/ppermute | solution.py:32
  385.6 53.2 %collective-permute-start.16 = (f32[320,512]{1,0:T(8,128)}, f32[320,512]{1,0:T(8,128)}, u32[]{:S(2)}, u32[]{:S(2)}) collective-permute-start(f32[320,512]{1,0:T(8,128)} %bitcast.185), channel_id=1, source_target_pairs={{6,0},{8,2},{10,4},{12,6},{14,8},{16,10},{18,12},{20,14},{22,16},{... | collective-permute-start | bytes 1966088 | tf_op jit(solution)/shard_map/ppermute | solution.py:32
  400.6 51.8 %collective-permute-start.17 = (f32[320,512]{1,0:T(8,128)}, f32[320,512]{1,0:T(8,128)}, u32[]{:S(2)}, u32[]{:S(2)}) collective-permute-start(f32[320,512]{1,0:T(8,128)} %bitcast.184), channel_id=1, source_target_pairs={{8,0},{10,2},{12,4},{14,6},{16,8},{18,10},{20,12},{22,14},{24,16},... | collective-permute-start | bytes 1966088 | tf_op jit(solution)/shard_map/ppermute | solution.py:32
  422.8 160.1 %collective-permute-start.21 = (f32[320,512]{1,0:T(8,128)}, f32[320,512]{1,0:T(8,128)}, u32[]{:S(2)}, u32[]{:S(2)}) collective-permute-start(f32[320,512]{1,0:T(8,128)} %bitcast.180), channel_id=1, source_target_pairs={{2,0},{4,2},{6,4},{8,6},{10,8},{12,10},{14,12},{16,14},{18,16},{20... | collective-permute-start | bytes 1966088 | tf_op jit(solution)/shard_map/ppermute | solution.py:32
  434.7 167.7 %collective-permute-start.22 = (f32[320,512]{1,0:T(8,128)}, f32[320,512]{1,0:T(8,128)}, u32[]{:S(2)}, u32[]{:S(2)}) collective-permute-start(f32[320,512]{1,0:T(8,128)} %bitcast.209), channel_id=1, source_target_pairs={{4,0},{6,2},{8,4},{10,6},{12,8},{14,10},{16,12},{18,14},{20,16},{2... | collective-permute-start | bytes 1966088 | tf_op jit(solution)/shard_map/ppermute | solution.py:32
  436.6 51.9 %collective-permute-start.18 = (f32[320,512]{1,0:T(8,128)}, f32[320,512]{1,0:T(8,128)}, u32[]{:S(2)}, u32[]{:S(2)}) collective-permute-start(f32[320,512]{1,0:T(8,128)} %bitcast.183), channel_id=1, source_target_pairs={{10,0},{12,2},{14,4},{16,6},{18,8},{20,10},{22,12},{24,14},{26,16}... | collective-permute-start | bytes 1966088 | tf_op jit(solution)/shard_map/ppermute | solution.py:32
  438.7 95.8 %collective-permute-start.19 = (f32[320,512]{1,0:T(8,128)}, f32[320,512]{1,0:T(8,128)}, u32[]{:S(2)}, u32[]{:S(2)}) collective-permute-start(f32[320,512]{1,0:T(8,128)} %bitcast.182), channel_id=1, source_target_pairs={{12,0},{14,2},{16,4},{18,6},{20,8},{22,10},{24,12},{26,14},{28,16}... | collective-permute-start | bytes 1966088 | tf_op jit(solution)/shard_map/ppermute | solution.py:32
  452.4 125.5 %collective-permute-start.20 = (f32[320,512]{1,0:T(8,128)}, f32[320,512]{1,0:T(8,128)}, u32[]{:S(2)}, u32[]{:S(2)}) collective-permute-start(f32[320,512]{1,0:T(8,128)} %bitcast.181), channel_id=1, source_target_pairs={{14,0},{16,2},{18,4},{20,6},{22,8},{24,10},{26,12},{28,14},{30,16}... | collective-permute-start | bytes 1966088 | tf_op jit(solution)/shard_map/ppermute | solution.py:32
  484.3 95.8 %copy-start.4 = (f32[4,40,8,128]{3,2,1,0:T(8,128)S(1)}, f32[4,40,8,128]{3,2,1,0:T(8,128)}, u32[]{:S(2)}) copy-start(f32[4,40,8,128]{3,2,1,0:T(8,128)} %get-tuple-element.162) | copy-start | bytes 1966084
  485.5 119.3 %copy-start = (f32[320,5120]{1,0:T(8,128)S(1)}, f32[320,5120]{1,0:T(8,128)}, u32[]{:S(2)}) copy-start(f32[320,5120]{1,0:T(8,128)} %fusion.41) | copy-start | bytes 19660804
  488.5 120.9 %collective-permute-start.23 = (f32[320,512]{1,0:T(8,128)S(1)}, f32[320,512]{1,0:T(8,128)S(1)}, u32[]{:S(2)}, u32[]{:S(2)}) collective-permute-start(f32[320,512]{1,0:T(8,128)S(1)} %bitcast.214), channel_id=1, source_target_pairs={{6,0},{8,2},{10,4},{12,6},{14,8},{16,10},{18,12},{20,14},{22,16},{... | collective-permute-start | bytes 1966088 | tf_op jit(solution)/shard_map/ppermute | solution.py:32
  534.6 74.7 %collective-permute-start.24 = (f32[320,512]{1,0:T(8,128)S(1)}, f32[320,512]{1,0:T(8,128)S(1)}, u32[]{:S(2)}, u32[]{:S(2)}) collective-permute-start(f32[320,512]{1,0:T(8,128)S(1)} %bitcast.213), channel_id=1, source_target_pairs={{8,0},{10,2},{12,4},{14,6},{16,8},{18,10},{20,12},{22,14},{24,16},... | collective-permute-start | bytes 1966088 | tf_op jit(solution)/shard_map/ppermute | solution.py:32
  577.9 31.5 %collective-permute-start.25 = (f32[320,512]{1,0:T(8,128)S(1)}, f32[320,512]{1,0:T(8,128)}, u32[]{:S(2)}, u32[]{:S(2)}) collective-permute-start(f32[320,512]{1,0:T(8,128)S(1)} %bitcast.212), channel_id=1, source_target_pairs={{10,0},{12,2},{14,4},{16,6},{18,8},{20,10},{22,12},{24,14},{26,16}... | collective-permute-start | bytes 1966088 | tf_op jit(solution)/shard_map/ppermute | solution.py:32
  582.9 34.8 %collective-permute-start.26 = (f32[320,512]{1,0:T(8,128)S(1)}, f32[320,512]{1,0:T(8,128)}, u32[]{:S(2)}, u32[]{:S(2)}) collective-permute-start(f32[320,512]{1,0:T(8,128)S(1)} %bitcast.211), channel_id=1, source_target_pairs={{12,0},{14,2},{16,4},{18,6},{20,8},{22,10},{24,12},{26,14},{28,16}... | collective-permute-start | bytes 1966088 | tf_op jit(solution)/shard_map/ppermute | solution.py:32
  602.4 29.4 %collective-permute-start.27 = (f32[320,512]{1,0:T(8,128)S(1)}, f32[320,512]{1,0:T(8,128)}, u32[]{:S(2)}, u32[]{:S(2)}) collective-permute-start(f32[320,512]{1,0:T(8,128)S(1)} %bitcast.210), channel_id=1, source_target_pairs={{14,0},{16,2},{18,4},{20,6},{22,8},{24,10},{26,12},{28,14},{30,16}... | collective-permute-start | bytes 1966088 | tf_op jit(solution)/shard_map/ppermute | solution.py:32
  (10 other events, 246.5 us)
Sparse Core Ops, SparseCore 0:
  638.1 82.8 reduce-scatter.1
where the time goes:
time: 737 us; the launch traced here: 728 us
  starting transfers between devices  229 us (31%)
  matrix products  179 us (24%)
  waiting for transfers between devices  106 us (14%)
  other arithmetic  71.9 us (10%)
  local copies, waits for them, and re-layouts  61.6 us (8%)
  loops' own time  51.3 us (7%)
  between operations  15.6 us (2%)
  blocking collectives  14 us (2%)
    ppermute x28, starting transfers between devices, from_behind(): return lax.ppermute(block, axis, route)  229 us
    reduce_scatter x1, waiting for transfers between devices, shards(): lax.psum_scatter(partial_input.astype(jnp.bfloat16), 'kv', scatter_dimens...  79.8 us
    convert_element_type x1, other arithmetic, shards(): score_gradient = (probs * (dprobs - delta)).astype(jnp.bfloat16)  51.8 us
    another operation x1, loops' own time, entering(): return lax.fori_loop(0, devices, step, start)  51.3 us
    dot_general x1, matrix products, shards(): jnp.einsum('tkgd,skd->kgts', grad_heads, value_heads, preferred_element_t...  47.4 us
    sub x1, matrix products, shards(): expo = jnp.where(allowed, jnp.exp(scores - top), 0.0)  41.9 us
    dot_general x1, matrix products, shards(): jnp.einsum('qwuh,uqwb->hqb', probability_narrow, grad_heads, preferred_el...  27.3 us
    ppermute x28, waiting for transfers between devices, from_behind(): return lax.ppermute(block, axis, route)  26.3 us
  transfers between devices with their start and end apart: 29, of which 5 were waited for; matrix products, arithmetic and copies ran while one was open for 24% of the time, Pallas kernels for 0%

commit v1 on v0

v1 whole, which is shorter than its diff:
```python
import functools

import jax
import jax.numpy as jnp
from jax import lax
from jax.experimental import pallas as pl
from jax.experimental.pallas import tpu as pltpu
from jax.sharding import PartitionSpec as P

QUERY_HEAD_COUNT = 40
KEY_VALUE_HEADS = 8
HEAD_SIZE = 128
GROUP_WIDTH = QUERY_HEAD_COUNT // KEY_VALUE_HEADS
REACH = 8
PLANE = 4
HEAD_CHUNKS = 2
SCALE = HEAD_SIZE ** (-0.5)
LOG2E = 1.4426950408889634
LOW = -1e30


def attention_kernel(
    info_ref, rows_ref, q_ref, g_ref, kv_ref, dq_ref, dkv_ref, s_ref, dp_ref, p_ref, ds_ref, stat_ref
):
    tok = kv_ref.shape[1]
    wide = q_ref.shape[0]
    lanes = []
    at = 0
    while at < wide:
        size = 512 if wide - at >= 1024 else wide - at
        lanes.append((at, size))
        at += size
    nt = (((1,), (1,)), ((), ()))
    tn = (((0,), (0,)), ((), ()))
    first_start = info_ref[REACH]
    last_start = info_ref[REACH + 1]

    stat_ref[0:1, :] = jnp.full((1, wide), LOW, jnp.float32)
    stat_ref[1:3, :] = jnp.zeros((2, wide), jnp.float32)

    def needed(slot):
        base = info_ref[slot]
        return (base >= 0) & (base + tok > first_start)

    def gather_stats(slot, masked):
        base = info_ref[slot]
        keys = kv_ref[slot, :, :HEAD_SIZE]
        values = kv_ref[slot, :, HEAD_SIZE:]
        for lo, size in lanes:
            cols = slice(lo, lo + size)
            s = lax.dot_general(
                keys, q_ref[cols, :], nt, preferred_element_type=jnp.float32
            ) * (SCALE * LOG2E)
            dp = lax.dot_general(values, g_ref[cols, :], nt, preferred_element_type=jnp.float32)
            if masked:
                pos = base + lax.broadcasted_iota(jnp.int32, (tok, size), 0)
                ok = (pos >= rows_ref[0:1, cols]) & (pos <= rows_ref[1:2, cols])
                s = jnp.where(ok, s, LOW)
            s_ref[slot, :, cols] = s
            dp_ref[slot, :, cols] = dp
            old = stat_ref[0:1, cols]
            new = jnp.maximum(old, jnp.max(s, axis=0, keepdims=True))
            fade = jnp.exp2(old - new)
            e = jnp.exp2(s - new)
            stat_ref[0:1, cols] = new
            stat_ref[1:2, cols] = stat_ref[1:2, cols] * fade + jnp.sum(e, axis=0, keepdims=True)
            stat_ref[2:3, cols] = stat_ref[2:3, cols] * fade + jnp.sum(
                e * dp, axis=0, keepdims=True
            )

    @pl.loop(0, REACH)
    def _(slot):
        whole = (slot > 0) & (info_ref[slot] >= last_start)

        @pl.when(needed(slot) & whole)
        def _():
            gather_stats(slot, False)

        @pl.when(needed(slot) & jnp.logical_not(whole))
        def _():
            gather_stats(slot, True)

    total = stat_ref[1:2, :]
    stat_ref[2:3, :] = stat_ref[2:3, :] / total
    stat_ref[0:1, :] = stat_ref[0:1, :] + jnp.log2(total)
    dq_ref[...] = jnp.zeros_like(dq_ref)

    @pl.loop(0, REACH)
    def _(slot):
        need = needed(slot)

        @pl.when(need)
        def _():
            keys = kv_ref[slot, :, :HEAD_SIZE]
            for lo, size in lanes:
                cols = slice(lo, lo + size)
                p = jnp.exp2(s_ref[slot, :, cols] - stat_ref[0:1, cols])
                p_ref[:, cols] = p.astype(jnp.bfloat16)
                ds = (p * (dp_ref[slot, :, cols] - stat_ref[2:3, cols])).astype(jnp.bfloat16)
                ds_ref[:, cols] = ds
                dq_ref[:, cols] += lax.dot_general(
                    keys, ds, tn, preferred_element_type=jnp.float32
                )
            dk = jnp.dot(ds_ref[...], q_ref[...], preferred_element_type=jnp.float32)
            dv = jnp.dot(p_ref[...], g_ref[...], preferred_element_type=jnp.float32)
            dkv_ref[slot, :, :HEAD_SIZE] = (dk * SCALE).astype(jnp.bfloat16)
            dkv_ref[slot, :, HEAD_SIZE:] = dv.astype(jnp.bfloat16)

        @pl.when(jnp.logical_not(need))
        def _():
            dkv_ref[slot] = jnp.zeros(dkv_ref.shape[1:], jnp.bfloat16)


def attention(info, rows, q_heads, g_heads, kv_slots, first):
    heads = kv_slots.shape[2] // (2 * HEAD_SIZE)
    tok = kv_slots.shape[1]
    wide = q_heads.shape[1]
    return pl.pallas_call(
        attention_kernel,
        grid=(heads,),
        in_specs=[
            pl.BlockSpec(memory_space=pltpu.SMEM),
            pl.BlockSpec((2, wide), lambda i: (0, 0)),
            pl.BlockSpec((None, wide, HEAD_SIZE), lambda i: (first + i, 0, 0)),
            pl.BlockSpec((None, wide, HEAD_SIZE), lambda i: (first + i, 0, 0)),
            pl.BlockSpec((REACH, tok, 2 * HEAD_SIZE), lambda i: (0, 0, i)),
        ],
        out_specs=[
            pl.BlockSpec((None, HEAD_SIZE, wide), lambda i: (i, 0, 0)),
            pl.BlockSpec((REACH, tok, 2 * HEAD_SIZE), lambda i: (0, 0, i)),
        ],
        out_shape=[
            jax.ShapeDtypeStruct((heads, HEAD_SIZE, wide), jnp.float32),
            jax.ShapeDtypeStruct(kv_slots.shape, jnp.bfloat16),
        ],
        scratch_shapes=[
            pltpu.VMEM((REACH, tok, wide), jnp.float32),
            pltpu.VMEM((REACH, tok, wide), jnp.float32),
            pltpu.VMEM((tok, wide), jnp.bfloat16),
            pltpu.VMEM((tok, wide), jnp.bfloat16),
            pltpu.VMEM((8, wide), jnp.float32),
        ],
        compiler_params=pltpu.CompilerParams(vmem_limit_bytes=56 * 1024 * 1024),
        cost_estimate=pl.CostEstimate(
            flops=heads * REACH * tok * wide * HEAD_SIZE * 20,
            bytes_accessed=heads * REACH * tok * HEAD_SIZE * 8,
            transcendentals=heads * REACH * tok * wide * 2,
        ),
    )(info, rows, q_heads, g_heads, kv_slots)


def shift(block, distance):
    devices = range(lax.axis_size("dc"))
    return lax.ppermute(
        block, "dc", [(i, i + distance) for i in devices if i + distance in devices]
    )


def swap(block, mask):
    return lax.ppermute(block, "dc", [(i, i ^ mask) for i in range(lax.axis_size("dc"))])


def shards(
    queries,
    keys,
    values,
    output_gradient,
    segment_ids,
    w_query,
    key_weight_matrix,
    value_weight_matrix,
):
    tok = queries.shape[0]
    kv_local = keys.shape[1] // HEAD_SIZE
    chunks = HEAD_CHUNKS if kv_local % HEAD_CHUNKS == 0 else 1
    wide = GROUP_WIDTH * tok
    me = lax.axis_index("dc")
    lane = lax.rem(me, PLANE)
    plane = me - lane
    f32 = jnp.float32

    pairs = jnp.concatenate(
        [keys.reshape(tok, kv_local, 1, HEAD_SIZE), values.reshape(tok, kv_local, 1, HEAD_SIZE)],
        axis=2,
    ).reshape(tok, chunks, -1)
    windows = []
    for c in range(chunks):
        own = pairs[:, c]
        near = shift(own, PLANE)
        far = shift(own, 2 * PLANE)
        slots = [own, near]
        for mask in range(1, PLANE):
            slots.append(swap(jnp.where(lane < (lane ^ mask), own, far), mask))
            slots.append(swap(near, mask))
        windows.append(jnp.stack(slots))

    bases = [me, me - PLANE]
    for mask in range(1, PLANE):
        other = lane ^ mask
        bases.append(jnp.where(other < lane, plane + other, plane - 2 * PLANE + other))
        bases.append(plane - PLANE + other)

    everyone = lax.all_gather(segment_ids, "dc", tiled=True)
    start = jnp.sum((everyone[None, :] < segment_ids[:, None]).astype(jnp.int32), axis=1)
    position = me * tok + jnp.arange(tok, dtype=jnp.int32)
    rows = jnp.tile(jnp.stack([start, position]), (1, GROUP_WIDTH))
    info = jnp.concatenate([jnp.stack(bases) * tok, start[:1], start[-1:]])

    def by_head(x):
        x = x.reshape(tok, kv_local, GROUP_WIDTH, HEAD_SIZE)
        return x.transpose(1, 2, 0, 3).reshape(kv_local, wide, HEAD_SIZE)

    q_heads = by_head(queries)
    g_heads = by_head(output_gradient)

    dq_parts = []
    totals = []
    per = kv_local // chunks
    for c in range(chunks):
        dq, parts = attention(info, rows, q_heads, g_heads, windows[c], c * per)
        dq_parts.append(dq)
        own = parts[0].astype(f32)
        near = parts[1].astype(f32)
        far = jnp.zeros_like(near)
        for mask in range(1, PLANE):
            back = swap(parts[2 * mask], mask).astype(f32)
            near = near + swap(parts[2 * mask + 1], mask).astype(f32)
            ahead = lane < (lane ^ mask)
            own = own + jnp.where(ahead, back, 0.0)
            far = far + jnp.where(ahead, 0.0, back)
        own = own + shift(near.astype(jnp.bfloat16), -PLANE).astype(f32)
        own = own + shift(far.astype(jnp.bfloat16), -2 * PLANE).astype(f32)
        totals.append(own.astype(jnp.bfloat16))
    total = jnp.concatenate(totals, axis=1).reshape(tok, kv_local, 2, HEAD_SIZE)
    key_grad = total[:, :, 0].reshape(tok, -1)
    value_grad = total[:, :, 1].reshape(tok, -1)
    dq = (jnp.concatenate(dq_parts, axis=0) * SCALE).astype(jnp.bfloat16)
    query_grad = (
        dq.reshape(kv_local, HEAD_SIZE, GROUP_WIDTH, tok).transpose(3, 0, 2, 1).reshape(tok, -1)
    )

    contract = (((1,), (1,)), ((), ()))
    dot = functools.partial(lax.dot_general, dimension_numbers=contract, preferred_element_type=f32)
    term = dot(query_grad, w_query)
    term = term + dot(key_grad, key_weight_matrix) + dot(value_grad, value_weight_matrix)
    term = term.astype(jnp.bfloat16)
    if lax.axis_size("kv") == 2:
        side = lax.axis_index("kv")
        half = term.shape[1] // 2
        mine = lax.dynamic_slice_in_dim(term, side * half, half, 1)
        theirs = lax.dynamic_slice_in_dim(term, (1 - side) * half, half, 1)
        got = lax.ppermute(theirs, "kv", [(0, 1), (1, 0)])
        input_grad = (mine.astype(f32) + got.astype(f32)).astype(jnp.bfloat16)
    else:
        input_grad = lax.psum_scatter(term, "kv", scatter_dimension=1, tiled=True)
    return (query_grad, key_grad, value_grad, input_grad)


def solution(mesh):
    in_specs = (
        P("dc", "kv"),
        P("dc", "kv"),
        P("dc", "kv"),
        P("dc", "kv"),
        P("dc"),
        P(None, "kv"),
        P(None, "kv"),
        P(None, "kv"),
    )
    out_specs = (P("dc", "kv"), P("dc", "kv"), P("dc", "kv"), P("dc", "kv"))
    return jax.shard_map(shards, mesh=mesh, in_specs=in_specs, out_specs=out_specs, check_vma=False)
```

time: 737 us -> 339 us (0.46); the launches traced: 728 us -> 338 us
  starting transfers between devices: 229 us -> 76.7 us
  matrix products: 179 us -> 27 us
  waiting for transfers between devices: 106 us -> 32.4 us
  blocking collectives: 14 us -> 76.3 us
  loops' own time: 51.3 us -> 0 us
  Pallas kernels: 0 us -> 50.4 us
  other arithmetic: 71.9 us -> 21.6 us
  between operations: 15.6 us -> 1.73 us
  local copies, waits for them, and re-layouts: 61.6 us -> 52.3 us
    ppermute x28 -> x33, starting transfers between devices: 229 us -> 76.7 us  [the longest x24 47.3 us: swap(): lax.ppermute(block, 'dc', [(i, i ^ mask) for i in range(lax.axis_size('dc...]
    dot_general x7 -> x3, matrix products: 137 us -> 27 us  [the longest x1 18.6 us: shards(): term = dot(query_grad, w_query)]
    reduce_scatter x1 -> x0, waiting for transfers between devices: 79.8 us -> none  [shards(): lax.psum_scatter(partial_input.astype(jnp.bfloat16), 'kv', scatter_dimens...]
    unnamed x1, blocking collectives: 14 us -> 76.3 us
    another operation x1 -> x0, loops' own time: 51.3 us -> none  [entering(): return lax.fori_loop(0, devices, step, start)]
    pallas_call x0 -> x2, Pallas kernels: none -> 50.4 us  [attention(): pl.pallas_call(attention_kernel, grid=(heads,), in_specs=[pl.BlockSpec(me...]
    convert_element_type x3 -> x7, other arithmetic: 56.9 us -> 13.4 us  [the longest x2 4.12 us: shards(): own = own + shift(near.astype(jnp.bfloat16), -PLANE).astype(f32)]
    sub x1 -> x0, matrix products: 41.9 us -> none  [shards(): expo = jnp.where(allowed, jnp.exp(scores - top), 0.0)]
  transfers between devices with their start and end apart: 29 -> 33, of which waited for: 5 -> 4; matrix products, arithmetic and copies ran while one was open for 24% -> 21% of each run, Pallas kernels for 0% -> 15%
where the time goes in v1:
time: 339 us; the launch traced here: 338 us
  starting transfers between devices  76.7 us (23%)
  blocking collectives  76.3 us (23%)
  local copies, waits for them, and re-layouts  52.3 us (15%)
  Pallas kernels  50.4 us (15%)
  waiting for transfers between devices  32.4 us (10%)
  matrix products  27 us (8%)
  other arithmetic  21.6 us (6%)
    unnamed x1, blocking collectives  76.3 us
    pallas_call x2, Pallas kernels, attention(): pl.pallas_call(attention_kernel, grid=(heads,), in_specs=[pl.BlockSpec(me...  50.4 us
    ppermute x24, starting transfers between devices, swap(): lax.ppermute(block, 'dc', [(i, i ^ mask) for i in range(lax.axis_size('dc...  47.3 us
    ppermute x24, waiting for transfers between devices, swap(): lax.ppermute(block, 'dc', [(i, i ^ mask) for i in range(lax.axis_size('dc...  32.4 us
    unnamed x44, local copies, waits for them, and re-layouts  23.1 us
    dot_general x1, matrix products, shards(): term = dot(query_grad, w_query)  18.6 us
    ppermute x1, starting transfers between devices, shards(): got = lax.ppermute(theirs, 'kv', [(0, 1), (1, 0)])  16.9 us
    ppermute x8, starting transfers between devices, shift(): lax.ppermute(block, 'dc', [(i, i + distance) for i in devices if i + dist...  12.5 us
  transfers between devices with their start and end apart: 33, of which 4 were waited for; matrix products, arithmetic and copies ran while one was open for 21% of the time, Pallas kernels for 15%

profile of v1, /device:TPU:25, one launch (start us, length us, event | category | flops | bytes accessed | tf_op | source)
XLA Modules:
  0.0 338.4 jit_solution(6876690272755538912)
XLA Ops:
  0.6 2.4 reshape.77
  3.0 2.4 reshape.78
  17.1 76.3 %all-reduce = s32[5120]{0:T(1024)S(1)} all-reduce(s32[5120]{0:T(1024)S(1)} %dynamic-update-slice), channel_id=1, replica_groups=mesh['dc'=16,'kv'=2] {'dc'}, use_global_device_ids=true, to_apply=%add | all-reduce | flops 5120 | bytes 40960
  96.3 3.6 %copy.29 = bf16[320,2560]{0,1:T(8,128)(2,1)S(1)} copy(bf16[320,2560]{1,0:T(8,128)(2,1)} %param.8) | data formatting | bytes 3276800 | tf_op args[0]
  99.9 2.3 copy.30
  102.2 3.6 %copy.31 = bf16[320,2560]{0,1:T(8,128)(2,1)S(1)} copy(bf16[320,2560]{1,0:T(8,128)(2,1)} %param.11) | data formatting | bytes 3276800 | tf_op args[3]
  105.8 2.3 copy.32
  108.2 2.1 pad_add_fusion.1.info_ref
  113.1 3.3 collective-permute-start.4
  123.1 7.6 %collective-permute-done.3 = bf16[320,512]{1,0:T(8,128)(2,1)S(1)} collective-permute-done((bf16[320,512]{1,0:T(8,128)(2,1)}, bf16[320,512]{1,0:T(8,128)(2,1)S(1)}, u32[]{:S(2)}, u32[]{:S(2)}) %collective-permute-start.3) | collective-permute-done | bytes 327712 | tf_op jit(solution)/shard_map/ppermute | solution.py:160
  133.2 14.6 %collective-permute-done.5 = bf16[320,512]{1,0:T(8,128)(2,1)S(1)} collective-permute-done((bf16[320,512]{1,0:T(8,128)(2,1)}, bf16[320,512]{1,0:T(8,128)(2,1)S(1)}, u32[]{:S(2)}, u32[]{:S(2)}) %collective-permute-start.5) | collective-permute-done | bytes 327712 | tf_op jit(solution)/shard_map/ppermute | solution.py:160
  149.6 6.6 %collective-permute-done.7 = bf16[320,512]{1,0:T(8,128)(2,1)S(1)} collective-permute-done((bf16[320,512]{1,0:T(8,128)(2,1)}, bf16[320,512]{1,0:T(8,128)(2,1)S(1)}, u32[]{:S(2)}, u32[]{:S(2)}) %collective-permute-start.7) | collective-permute-done | bytes 327712 | tf_op jit(solution)/shard_map/ppermute | solution.py:160
  158.6 25.2 %shard_map.111 = (f32[2,128,1600]{2,1,0:T(8,128)}, bf16[8,320,512]{2,1,0:T(8,128)(2,1)}) custom-call(s32[10]{0:T(128)} %pad_add_fusion.1.info_ref, s32[2,1600]{1,0:T(2,128)} %tile.10.rows_ref, bf16[4,1600,128]{2,1,0:T(8,128)(2,1)} %bitcast.120, bf16[4,1600,128]{2,1,0:T(8,128)(2,1)} %bitcast.122, bf16[8,320,512]{2,1,0:T(8,128)(2,1)} %copy-done.6), custom_call_target="tpu_custom_call" | custom-call | flops 20971520000 | bytes 5242880 | tf_op jit(solution)/shard_map/pallas_call | solution.py:118
  183.8 2.7 slice_bitcast_fusion.8
  186.6 11.7 %collective-permute-start.15 = (bf16[320,512]{1,0:T(8,128)(2,1)}, bf16[320,512]{1,0:T(8,128)(2,1)S(1)}, u32[]{:S(2)}, u32[]{:S(2)}) collective-permute-start(bf16[320,512]{1,0:T(8,128)(2,1)} %collective-permute-done.8), channel_id=1, source_target_pairs={{0,6},{2,4},{4,2},{6,0},{8,14},{10,12},{12,10},{14,8},{16,22},{18,... | collective-permute-start | bytes 983048 | tf_op jit(solution)/shard_map/ppermute | solution.py:160
  200.8 2.4 collective-permute-start.21
  205.7 25.2 %shard_map.112 = (f32[2,128,1600]{2,1,0:T(8,128)}, bf16[8,320,512]{2,1,0:T(8,128)(2,1)}) custom-call(s32[10]{0:T(128)} %pad_add_fusion.1.info_ref, s32[2,1600]{1,0:T(2,128)} %tile.10.rows_ref, bf16[4,1600,128]{2,1,0:T(8,128)(2,1)} %bitcast.121, bf16[4,1600,128]{2,1,0:T(8,128)(2,1)} %bitcast.123, bf16[8,320,512]{2,1,0:T(8,128)(2,1)} %bitcast_dynamic-update-slice_fusion.kv_ref), custom_call_target="tpu_custom_call" | custom-call | flops 20971520000 | bytes 5242880 | tf_op jit(solution)/shard_map/pallas_call | solution.py:118
  233.6 2.8 slice_bitcast_fusion.2
  236.3 14.4 %collective-permute-start.18 = (bf16[320,512]{1,0:T(8,128)(2,1)}, bf16[320,512]{1,0:T(8,128)(2,1)}, u32[]{:S(2)}, u32[]{:S(2)}) collective-permute-start(bf16[320,512]{1,0:T(8,128)(2,1)} %get-tuple-element.25), channel_id=1, source_target_pairs={{0,6},{2,4},{4,2},{6,0},{8,14},{10,12},{12,10},{14,8},{16,22},{18,... | collective-permute-start | bytes 983048 | tf_op jit(solution)/shard_map/ppermute | solution.py:160
  252.4 2.8 copy.39
  255.6 2.3 collective-permute-start.29
  257.9 2.2 fusion.26
  260.4 2.3 collective-permute-start.26
  262.7 2.1 fusion.11
  272.1 3.5 %collective-permute-done.25 = bf16[320,512]{1,0:T(8,128)(2,1)S(1)} collective-permute-done((bf16[320,512]{1,0:T(8,128)(2,1)}, bf16[320,512]{1,0:T(8,128)(2,1)S(1)}, u32[]{:S(2)}, u32[]{:S(2)}) %collective-permute-start.25) | collective-permute-done | bytes 327712 | tf_op jit(solution)/shard_map/ppermute | solution.py:160
  276.5 2.0 collective-permute-start.31
  278.6 18.6 %fusion.29 = f32[320,5120]{1,0:T(8,128)} fusion(bf16[320,2560]{0,1:T(8,128)(2,1)S(1)} %bitcast.112, bf16[5120,2560]{1,0:T(8,128)(2,1)} %param.13), kind=kOutput, calls=%fused_computation.95 | convolution fusion | flops 8388608000 | bytes 34406400 | tf_op jit(solution)/shard_map/dot_general | solution.py:244
  300.9 3.7 %slice_reduce_fusion = (bf16[320,4,128]{2,1,0:T(4,128)(2,1)S(1)}, bf16[320,4,128]{2,1,0:T(4,128)(2,1)S(1)}) fusion(bf16[320,4,2,128]{3,2,1,0:T(2,128)(2,1)S(1)} %reshape.67), kind=kLoop, calls=%fused_computation.38 | loop fusion | bytes 1310720 | tf_op jit(solution)/shard_map/slice | solution.py:236
  304.8 6.6 %convolution_add_fusion.1 = f32[320,5120]{1,0:T(8,128)S(1)} fusion(f32[320,5120]{1,0:T(8,128)} %fusion.29, bf16[320,512]{1,0:T(8,128)(2,1)S(1)} %get-tuple-element.45, bf16[5120,512]{1,0:T(8,128)(2,1)} %param.14), kind=kOutput, calls=%fused_computation.1 | convolution fusion | flops 1679360000 | bytes 18677760 | tf_op jit(solution)/shard_map/dot_general | solution.py:245
  314.6 16.9 %collective-permute-start.32 = (bf16[320,2560]{1,0:T(8,128)(2,1)}, bf16[320,2560]{1,0:T(8,128)(2,1)}, u32[]{:S(2)}, u32[]{:S(2)}) collective-permute-start(bf16[320,2560]{1,0:T(8,128)(2,1)} %constant_dynamic-slice_fusion), channel_id=1, source_target_pairs={{0,1},{1,0},{2,3},{3,2},{4,5},{5,4},{6,7},{7,6},{8,9},{9,8},{10,11... | collective-permute-start | bytes 4915208 | tf_op jit(solution)/shard_map/ppermute | solution.py:252
  331.4 3.9 %copy.42 = bf16[320,2560]{1,0:T(8,128)(2,1)} copy(bf16[320,2560]{0,1:T(8,128)(2,1)} %bitcast.113) | data formatting | bytes 3276800
  335.3 3.1 add_convert_fusion
  (124 shorter events, 55.5 us)
Async XLA Ops:
  8.8 101.5 %collective-permute-start.1 = (bf16[320,512]{1,0:T(8,128)(2,1)}, bf16[320,512]{1,0:T(8,128)(2,1)}, u32[]{:S(2)}, u32[]{:S(2)}) collective-permute-start(bf16[320,512]{1,0:T(8,128)(2,1)} %bitcast.111), channel_id=1, source_target_pairs={{0,16},{2,18},{4,20},{6,22},{8,24},{10,26},{12,28},{14,30},{1,17},... | collective-permute-start | bytes 983048 | tf_op jit(solution)/shard_map/ppermute | solution.py:154
  10.1 107.3 %collective-permute-start = (bf16[320,512]{1,0:T(8,128)(2,1)}, bf16[320,512]{1,0:T(8,128)(2,1)}, u32[]{:S(2)}, u32[]{:S(2)}) collective-permute-start(bf16[320,512]{1,0:T(8,128)(2,1)} %bitcast.111), channel_id=1, source_target_pairs={{0,8},{2,10},{4,12},{6,14},{8,16},{10,18},{12,20},{14,22},{16,24},... | collective-permute-start | bytes 983048 | tf_op jit(solution)/shard_map/ppermute | solution.py:154
  12.2 104.2 %collective-permute-start.9 = (bf16[320,512]{1,0:T(8,128)(2,1)}, bf16[320,512]{1,0:T(8,128)(2,1)}, u32[]{:S(2)}, u32[]{:S(2)}) collective-permute-start(bf16[320,512]{1,0:T(8,128)(2,1)} %bitcast.110), channel_id=1, source_target_pairs={{0,16},{2,18},{4,20},{6,22},{8,24},{10,26},{12,28},{14,30},{1,17},... | collective-permute-start | bytes 983048 | tf_op jit(solution)/shard_map/ppermute | solution.py:154
  13.5 106.2 %collective-permute-start.8 = (bf16[320,512]{1,0:T(8,128)(2,1)}, bf16[320,512]{1,0:T(8,128)(2,1)}, u32[]{:S(2)}, u32[]{:S(2)}) collective-permute-start(bf16[320,512]{1,0:T(8,128)(2,1)} %bitcast.110), channel_id=1, source_target_pairs={{0,8},{2,10},{4,12},{6,14},{8,16},{10,18},{12,20},{14,22},{16,24},... | collective-permute-start | bytes 983048 | tf_op jit(solution)/shard_map/ppermute | solution.py:154
  111.4 10.4 %collective-permute-start.2 = (bf16[320,512]{1,0:T(8,128)(2,1)S(1)}, bf16[320,512]{1,0:T(8,128)(2,1)S(1)}, u32[]{:S(2)}, u32[]{:S(2)}) collective-permute-start(bf16[320,512]{1,0:T(8,128)(2,1)S(1)} %get-tuple-element.36), channel_id=1, source_target_pairs={{0,2},{2,0},{4,6},{6,4},{8,10},{10,8},{12,14},{14,12},{16,18},{18,... | collective-permute-start | bytes 983048 | tf_op jit(solution)/shard_map/ppermute | solution.py:160
  113.1 19.2 %collective-permute-start.4 = (bf16[320,512]{1,0:T(8,128)(2,1)S(1)}, bf16[320,512]{1,0:T(8,128)(2,1)S(1)}, u32[]{:S(2)}, u32[]{:S(2)}) collective-permute-start(bf16[320,512]{1,0:T(8,128)(2,1)S(1)} %get-tuple-element.35), channel_id=1, source_target_pairs={{0,4},{2,6},{4,0},{6,2},{8,12},{10,14},{12,8},{14,10},{16,20},{18,... | collective-permute-start | bytes 983048 | tf_op jit(solution)/shard_map/ppermute | solution.py:160
  116.4 32.2 %collective-permute-start.6 = (bf16[320,512]{1,0:T(8,128)(2,1)S(1)}, bf16[320,512]{1,0:T(8,128)(2,1)S(1)}, u32[]{:S(2)}, u32[]{:S(2)}) collective-permute-start(bf16[320,512]{1,0:T(8,128)(2,1)S(1)} %get-tuple-element.34), channel_id=1, source_target_pairs={{0,6},{2,4},{4,2},{6,0},{8,14},{10,12},{12,10},{14,8},{16,22},{18,... | collective-permute-start | bytes 983048 | tf_op jit(solution)/shard_map/ppermute | solution.py:160
  117.5 69.1 %collective-permute-start.10 = (bf16[320,512]{1,0:T(8,128)(2,1)S(1)}, bf16[320,512]{1,0:T(8,128)(2,1)S(1)}, u32[]{:S(2)}, u32[]{:S(2)}) collective-permute-start(bf16[320,512]{1,0:T(8,128)(2,1)S(1)} %get-tuple-element.41), channel_id=1, source_target_pairs={{0,2},{2,0},{4,6},{6,4},{8,10},{10,8},{12,14},{14,12},{16,18},{18,... | collective-permute-start | bytes 983048 | tf_op jit(solution)/shard_map/ppermute | solution.py:160
  119.7 11.0 %collective-permute-start.3 = (bf16[320,512]{1,0:T(8,128)(2,1)}, bf16[320,512]{1,0:T(8,128)(2,1)S(1)}, u32[]{:S(2)}, u32[]{:S(2)}) collective-permute-start(bf16[320,512]{1,0:T(8,128)(2,1)} %collective-permute-done), channel_id=1, source_target_pairs={{0,2},{2,0},{4,6},{6,4},{8,10},{10,8},{12,14},{14,12},{16,18},{18,... | collective-permute-start | bytes 983048 | tf_op jit(solution)/shard_map/ppermute | solution.py:160
  121.8 77.9 %collective-permute-start.12 = (bf16[320,512]{1,0:T(8,128)(2,1)S(1)}, bf16[320,512]{1,0:T(8,128)(2,1)S(1)}, u32[]{:S(2)}, u32[]{:S(2)}) collective-permute-start(bf16[320,512]{1,0:T(8,128)(2,1)S(1)} %get-tuple-element.40), channel_id=1, source_target_pairs={{0,4},{2,6},{4,0},{6,2},{8,12},{10,14},{12,8},{14,10},{16,20},{18,... | collective-permute-start | bytes 983048 | tf_op jit(solution)/shard_map/ppermute | solution.py:160
  130.7 17.2 %collective-permute-start.5 = (bf16[320,512]{1,0:T(8,128)(2,1)}, bf16[320,512]{1,0:T(8,128)(2,1)S(1)}, u32[]{:S(2)}, u32[]{:S(2)}) collective-permute-start(bf16[320,512]{1,0:T(8,128)(2,1)} %collective-permute-done), channel_id=1, source_target_pairs={{0,4},{2,6},{4,0},{6,2},{8,12},{10,14},{12,8},{14,10},{16,20},{18,... | collective-permute-start | bytes 983048 | tf_op jit(solution)/shard_map/ppermute | solution.py:160
  132.3 71.5 %collective-permute-start.14 = (bf16[320,512]{1,0:T(8,128)(2,1)S(1)}, bf16[320,512]{1,0:T(8,128)(2,1)S(1)}, u32[]{:S(2)}, u32[]{:S(2)}) collective-permute-start(bf16[320,512]{1,0:T(8,128)(2,1)S(1)} %get-tuple-element.39), channel_id=1, source_target_pairs={{0,6},{2,4},{4,2},{6,0},{8,14},{10,12},{12,10},{14,8},{16,22},{18,... | collective-permute-start | bytes 983048 | tf_op jit(solution)/shard_map/ppermute | solution.py:160
  148.6 50.4 %collective-permute-start.11 = (bf16[320,512]{1,0:T(8,128)(2,1)}, bf16[320,512]{1,0:T(8,128)(2,1)S(1)}, u32[]{:S(2)}, u32[]{:S(2)}) collective-permute-start(bf16[320,512]{1,0:T(8,128)(2,1)} %collective-permute-done.8), channel_id=1, source_target_pairs={{0,2},{2,0},{4,6},{6,4},{8,10},{10,8},{12,14},{14,12},{16,18},{18,... | collective-permute-start | bytes 983048 | tf_op jit(solution)/shard_map/ppermute | solution.py:160
  156.2 44.5 %collective-permute-start.13 = (bf16[320,512]{1,0:T(8,128)(2,1)}, bf16[320,512]{1,0:T(8,128)(2,1)S(1)}, u32[]{:S(2)}, u32[]{:S(2)}) collective-permute-start(bf16[320,512]{1,0:T(8,128)(2,1)} %collective-permute-done.8), channel_id=1, source_target_pairs={{0,4},{2,6},{4,0},{6,2},{8,12},{10,14},{12,8},{14,10},{16,20},{18,... | collective-permute-start | bytes 983048 | tf_op jit(solution)/shard_map/ppermute | solution.py:160
  186.6 18.1 %collective-permute-start.15 = (bf16[320,512]{1,0:T(8,128)(2,1)}, bf16[320,512]{1,0:T(8,128)(2,1)S(1)}, u32[]{:S(2)}, u32[]{:S(2)}) collective-permute-start(bf16[320,512]{1,0:T(8,128)(2,1)} %collective-permute-done.8), channel_id=1, source_target_pairs={{0,6},{2,4},{4,2},{6,0},{8,14},{10,12},{12,10},{14,8},{16,22},{18,... | collective-permute-start | bytes 983048 | tf_op jit(solution)/shard_map/ppermute | solution.py:160
  199.0 37.4 %collective-permute-start.19 = (bf16[320,512]{1,0:T(8,128)(2,1)}, bf16[320,512]{1,0:T(8,128)(2,1)}, u32[]{:S(2)}, u32[]{:S(2)}) collective-permute-start(bf16[320,512]{1,0:T(8,128)(2,1)} %get-tuple-element.22), channel_id=1, source_target_pairs={{0,2},{2,0},{4,6},{6,4},{8,10},{10,8},{12,14},{14,12},{16,18},{18,... | collective-permute-start | bytes 983048 | tf_op jit(solution)/shard_map/ppermute | solution.py:160
  199.7 51.1 %collective-permute-start.20 = (bf16[320,512]{1,0:T(8,128)(2,1)}, bf16[320,512]{1,0:T(8,128)(2,1)}, u32[]{:S(2)}, u32[]{:S(2)}) collective-permute-start(bf16[320,512]{1,0:T(8,128)(2,1)} %get-tuple-element.24), channel_id=1, source_target_pairs={{0,4},{2,6},{4,0},{6,2},{8,12},{10,14},{12,8},{14,10},{16,20},{18,... | collective-permute-start | bytes 983048 | tf_op jit(solution)/shard_map/ppermute | solution.py:160
  200.8 54.4 %collective-permute-start.21 = (bf16[320,512]{1,0:T(8,128)(2,1)}, bf16[320,512]{1,0:T(8,128)(2,1)}, u32[]{:S(2)}, u32[]{:S(2)}) collective-permute-start(bf16[320,512]{1,0:T(8,128)(2,1)} %get-tuple-element.23), channel_id=1, source_target_pairs={{0,6},{2,4},{4,2},{6,0},{8,14},{10,12},{12,10},{14,8},{16,22},{18,... | collective-permute-start | bytes 983048 | tf_op jit(solution)/shard_map/ppermute | solution.py:160
  203.9 51.7 %collective-permute-start.16 = (bf16[320,512]{1,0:T(8,128)(2,1)}, bf16[320,512]{1,0:T(8,128)(2,1)}, u32[]{:S(2)}, u32[]{:S(2)}) collective-permute-start(bf16[320,512]{1,0:T(8,128)(2,1)} %get-tuple-element.27), channel_id=1, source_target_pairs={{0,2},{2,0},{4,6},{6,4},{8,10},{10,8},{12,14},{14,12},{16,18},{18,... | collective-permute-start | bytes 983048 | tf_op jit(solution)/shard_map/ppermute | solution.py:160
  204.7 55.4 %collective-permute-start.17 = (bf16[320,512]{1,0:T(8,128)(2,1)}, bf16[320,512]{1,0:T(8,128)(2,1)}, u32[]{:S(2)}, u32[]{:S(2)}) collective-permute-start(bf16[320,512]{1,0:T(8,128)(2,1)} %get-tuple-element.26), channel_id=1, source_target_pairs={{0,4},{2,6},{4,0},{6,2},{8,12},{10,14},{12,8},{14,10},{16,20},{18,... | collective-permute-start | bytes 983048 | tf_op jit(solution)/shard_map/ppermute | solution.py:160
  236.3 23.7 %collective-permute-start.18 = (bf16[320,512]{1,0:T(8,128)(2,1)}, bf16[320,512]{1,0:T(8,128)(2,1)}, u32[]{:S(2)}, u32[]{:S(2)}) collective-permute-start(bf16[320,512]{1,0:T(8,128)(2,1)} %get-tuple-element.25), channel_id=1, source_target_pairs={{0,6},{2,4},{4,2},{6,0},{8,14},{10,12},{12,10},{14,8},{16,22},{18,... | collective-permute-start | bytes 983048 | tf_op jit(solution)/shard_map/ppermute | solution.py:160
  250.8 9.7 %collective-permute-start.27 = (bf16[320,512]{1,0:T(8,128)(2,1)}, bf16[320,512]{1,0:T(8,128)(2,1)}, u32[]{:S(2)}, u32[]{:S(2)}) collective-permute-start(bf16[320,512]{1,0:T(8,128)(2,1)} %get-tuple-element.28), channel_id=1, source_target_pairs={{0,2},{2,0},{4,6},{6,4},{8,10},{10,8},{12,14},{14,12},{16,18},{18,... | collective-permute-start | bytes 983048 | tf_op jit(solution)/shard_map/ppermute | solution.py:160
  255.2 9.6 %collective-permute-start.28 = (bf16[320,512]{1,0:T(8,128)(2,1)S(1)}, bf16[320,512]{1,0:T(8,128)(2,1)S(1)}, u32[]{:S(2)}, u32[]{:S(2)}) collective-permute-start(bf16[320,512]{1,0:T(8,128)(2,1)S(1)} %copy-done.4), channel_id=1, source_target_pairs={{0,4},{2,6},{4,0},{6,2},{8,12},{10,14},{12,8},{14,10},{16,20},{18,... | collective-permute-start | bytes 983048 | tf_op jit(solution)/shard_map/ppermute | solution.py:160
  255.6 10.5 %collective-permute-start.29 = (bf16[320,512]{1,0:T(8,128)(2,1)}, bf16[320,512]{1,0:T(8,128)(2,1)S(1)}, u32[]{:S(2)}, u32[]{:S(2)}) collective-permute-start(bf16[320,512]{1,0:T(8,128)(2,1)} %get-tuple-element.29), channel_id=1, source_target_pairs={{0,6},{2,4},{4,2},{6,0},{8,14},{10,12},{12,10},{14,8},{16,22},{18,... | collective-permute-start | bytes 983048 | tf_op jit(solution)/shard_map/ppermute | solution.py:160
  260.1 10.0 %collective-permute-start.24 = (bf16[320,512]{1,0:T(8,128)(2,1)}, bf16[320,512]{1,0:T(8,128)(2,1)S(1)}, u32[]{:S(2)}, u32[]{:S(2)}) collective-permute-start(bf16[320,512]{1,0:T(8,128)(2,1)} %get-tuple-element.33), channel_id=1, source_target_pairs={{0,2},{2,0},{4,6},{6,4},{8,10},{10,8},{12,14},{14,12},{16,18},{18,... | collective-permute-start | bytes 983048 | tf_op jit(solution)/shard_map/ppermute | solution.py:160
  260.1 15.5 %collective-permute-start.25 = (bf16[320,512]{1,0:T(8,128)(2,1)}, bf16[320,512]{1,0:T(8,128)(2,1)S(1)}, u32[]{:S(2)}, u32[]{:S(2)}) collective-permute-start(bf16[320,512]{1,0:T(8,128)(2,1)} %get-tuple-element.32), channel_id=1, source_target_pairs={{0,4},{2,6},{4,0},{6,2},{8,12},{10,14},{12,8},{14,10},{16,20},{18,... | collective-permute-start | bytes 983048 | tf_op jit(solution)/shard_map/ppermute | solution.py:160
  260.4 15.2 %collective-permute-start.26 = (bf16[320,512]{1,0:T(8,128)(2,1)}, bf16[320,512]{1,0:T(8,128)(2,1)S(1)}, u32[]{:S(2)}, u32[]{:S(2)}) collective-permute-start(bf16[320,512]{1,0:T(8,128)(2,1)} %get-tuple-element.31), channel_id=1, source_target_pairs={{0,6},{2,4},{4,2},{6,0},{8,14},{10,12},{12,10},{14,8},{16,22},{18,... | collective-permute-start | bytes 983048 | tf_op jit(solution)/shard_map/ppermute | solution.py:160
  264.8 32.3 %collective-permute-start.22 = (bf16[320,512]{1,0:T(8,128)(2,1)}, bf16[320,512]{1,0:T(8,128)(2,1)S(1)}, u32[]{:S(2)}, u32[]{:S(2)}) collective-permute-start(bf16[320,512]{1,0:T(8,128)(2,1)} %fusion.26), channel_id=1, source_target_pairs={{8,0},{10,2},{12,4},{14,6},{16,8},{18,10},{20,12},{22,14},{24,16},... | collective-permute-start | bytes 983048 | tf_op jit(solution)/shard_map/ppermute | solution.py:154
  266.1 31.0 %collective-permute-start.23 = (bf16[320,512]{1,0:T(8,128)(2,1)}, bf16[320,512]{1,0:T(8,128)(2,1)}, u32[]{:S(2)}, u32[]{:S(2)}) collective-permute-start(bf16[320,512]{1,0:T(8,128)(2,1)} %fusion.11), channel_id=1, source_target_pairs={{16,0},{18,2},{20,4},{22,6},{24,8},{26,10},{28,12},{30,14},{17,1},... | collective-permute-start | bytes 983048 | tf_op jit(solution)/shard_map/ppermute | solution.py:154
  270.1 28.7 %collective-permute-start.30 = (bf16[320,512]{1,0:T(8,128)(2,1)}, bf16[320,512]{1,0:T(8,128)(2,1)}, u32[]{:S(2)}, u32[]{:S(2)}) collective-permute-start(bf16[320,512]{1,0:T(8,128)(2,1)} %fusion.23), channel_id=1, source_target_pairs={{8,0},{10,2},{12,4},{14,6},{16,8},{18,10},{20,12},{22,14},{24,16},... | collective-permute-start | bytes 983048 | tf_op jit(solution)/shard_map/ppermute | solution.py:154
  276.5 22.3 %collective-permute-start.31 = (bf16[320,512]{1,0:T(8,128)(2,1)}, bf16[320,512]{1,0:T(8,128)(2,1)}, u32[]{:S(2)}, u32[]{:S(2)}) collective-permute-start(bf16[320,512]{1,0:T(8,128)(2,1)} %fusion.20), channel_id=1, source_target_pairs={{16,0},{18,2},{20,4},{22,6},{24,8},{26,10},{28,12},{30,14},{17,1},... | collective-permute-start | bytes 983048 | tf_op jit(solution)/shard_map/ppermute | solution.py:154
  314.6 20.7 %collective-permute-start.32 = (bf16[320,2560]{1,0:T(8,128)(2,1)}, bf16[320,2560]{1,0:T(8,128)(2,1)}, u32[]{:S(2)}, u32[]{:S(2)}) collective-permute-start(bf16[320,2560]{1,0:T(8,128)(2,1)} %constant_dynamic-slice_fusion), channel_id=1, source_target_pairs={{0,1},{1,0},{2,3},{3,2},{4,5},{5,4},{6,7},{7,6},{8,9},{9,8},{10,11... | collective-permute-start | bytes 4915208 | tf_op jit(solution)/shard_map/ppermute | solution.py:252
  (12 other events, 120.1 us)

commit v2 on v1

--- a/solution.py
+++ b/solution.py
@@ -200,8 +200,17 @@
         bases.append(jnp.where(other < lane, plane + other, plane - 2 * PLANE + other))
         bases.append(plane - PLANE + other)
 
-    everyone = lax.all_gather(segment_ids, "dc", tiled=True)
-    start = jnp.sum((everyone[None, :] < segment_ids[:, None]).astype(jnp.int32), axis=1)
+    own_segs = segment_ids[None, :]
+    near_segs = shift(own_segs, PLANE)
+    far_segs = shift(own_segs, 2 * PLANE)
+    seg_slots = [own_segs, near_segs]
+    for mask in range(1, PLANE):
+        first = jnp.where(lane < (lane ^ mask), own_segs, far_segs)
+        seg_slots.append(swap(jnp.concatenate([first, near_segs]), mask))
+    window_segs = jnp.concatenate(seg_slots)
+    window_segs = jnp.where(jnp.stack(bases)[:, None] < 0, -1, window_segs).reshape(-1)
+    earlier = (window_segs[None, :] < segment_ids[:, None]).astype(jnp.int32)
+    start = (me - REACH + 1) * tok + jnp.sum(earlier, axis=1)
     position = me * tok + jnp.arange(tok, dtype=jnp.int32)
     rows = jnp.tile(jnp.stack([start, position]), (1, GROUP_WIDTH))
     info = jnp.concatenate([jnp.stack(bases) * tok, start[:1], start[-1:]])

time: 339 us -> 299 us (0.88)
  blocking collectives: 76.3 us -> 0 us
  waiting for transfers between devices: 32.4 us -> 81.4 us
  starting transfers between devices: 76.7 us -> 67.7 us
    unnamed x1 -> x0, blocking collectives: 76.3 us -> none
    ppermute x8 -> x10, waiting for transfers between devices: 0.02 us -> 28.3 us  [shift(): lax.ppermute(block, 'dc', [(i, i + distance) for i in devices if i + dist...]
    ppermute x24 -> x27, waiting for transfers between devices: 32.4 us -> 53.1 us  [swap(): lax.ppermute(block, 'dc', [(i, i ^ mask) for i in range(lax.axis_size('dc...]
    ppermute x1, starting transfers between devices: 16.9 us -> 2.05 us  [shards(): got = lax.ppermute(theirs, 'kv', [(0, 1), (1, 0)])]
    ppermute x24 -> x27, starting transfers between devices: 47.3 us -> 50.4 us  [swap(): lax.ppermute(block, 'dc', [(i, i ^ mask) for i in range(lax.axis_size('dc...]
    ppermute x8 -> x10, starting transfers between devices: 12.5 us -> 15.3 us  [shift(): lax.ppermute(block, 'dc', [(i, i + distance) for i in devices if i + dist...]
    unnamed x44 -> x39, local copies, waits for them, and re-layouts: 23.1 us -> 21.3 us
  transfers between devices with their start and end apart: 33 -> 38, of which waited for: 4 -> 7; matrix products, arithmetic and copies ran while one was open for 21% -> 23% of each run, Pallas kernels for 15% -> 17%
where the time goes in v2:
time: 299 us; the launch traced here: 298 us
  waiting for transfers between devices  81.4 us (27%)
  starting transfers between devices  67.7 us (23%)
  local copies, waits for them, and re-layouts  50.3 us (17%)
  Pallas kernels  50.2 us (17%)
  matrix products  27 us (9%)
  other arithmetic  20.3 us (7%)
    ppermute x27, waiting for transfers between devices, swap(): lax.ppermute(block, 'dc', [(i, i ^ mask) for i in range(lax.axis_size('dc...  53.1 us
    ppermute x27, starting transfers between devices, swap(): lax.ppermute(block, 'dc', [(i, i ^ mask) for i in range(lax.axis_size('dc...  50.4 us
    pallas_call x2, Pallas kernels, attention(): pl.pallas_call(attention_kernel, grid=(heads,), in_specs=[pl.BlockSpec(me...  50.2 us
    ppermute x10, waiting for transfers between devices, shift(): lax.ppermute(block, 'dc', [(i, i + distance) for i in devices if i + dist...  28.3 us
    unnamed x39, local copies, waits for them, and re-layouts  21.3 us
    dot_general x1, matrix products, shards(): term = dot(query_grad, w_query)  18.5 us
    ppermute x10, starting transfers between devices, shift(): lax.ppermute(block, 'dc', [(i, i + distance) for i in devices if i + dist...  15.3 us
    dot_general x1, matrix products, shards(): dot(key_grad, key_weight_matrix)  6.55 us
  transfers between devices with their start and end apart: 38, of which 7 were waited for; matrix products, arithmetic and copies ran while one was open for 23% of the time, Pallas kernels for 17%

profile of v2, /device:TPU:25, one launch (start us, length us, event | category | flops | bytes accessed | tf_op | source)
XLA Modules:
  0.0 298.2 jit_solution(9966156588361151091)
XLA Ops:
  0.6 2.4 reshape.159
  3.0 2.4 reshape.160
  15.7 19.5 %collective-permute-done.1 = s32[1,320]{1,0:T(1,128)S(1)} collective-permute-done((s32[1,320]{1,0:T(1,128)S(1)}, s32[1,320]{1,0:T(1,128)S(1)}, u32[]{:S(2)}, u32[]{:S(2)}) %collective-permute-start.1) | collective-permute-done | bytes 1312 | tf_op jit(solution)/shard_map/ppermute | solution.py:154
  38.7 3.6 %copy.29 = bf16[320,2560]{0,1:T(8,128)(2,1)S(1)} copy(bf16[320,2560]{1,0:T(8,128)(2,1)} %param.8) | data formatting | bytes 3276800 | tf_op args[0]
  42.3 2.3 copy.30
  44.6 3.6 %copy.31 = bf16[320,2560]{0,1:T(8,128)(2,1)S(1)} copy(bf16[320,2560]{1,0:T(8,128)(2,1)} %param.11) | data formatting | bytes 3276800 | tf_op args[3]
  48.2 2.3 copy.32
  60.9 8.8 %collective-permute-done.14 = bf16[320,512]{1,0:T(8,128)(2,1)S(1)} collective-permute-done((bf16[320,512]{1,0:T(8,128)(2,1)}, bf16[320,512]{1,0:T(8,128)(2,1)S(1)}, u32[]{:S(2)}, u32[]{:S(2)}) %collective-permute-start.14) | collective-permute-done | bytes 327712 | tf_op jit(solution)/shard_map/ppermute | solution.py:154
  69.7 2.2 collective-permute-start.11
  75.6 16.8 %collective-permute-done.8 = bf16[320,512]{1,0:T(8,128)(2,1)S(1)} collective-permute-done((bf16[320,512]{1,0:T(8,128)(2,1)}, bf16[320,512]{1,0:T(8,128)(2,1)S(1)}, u32[]{:S(2)}, u32[]{:S(2)}) %collective-permute-start.8) | collective-permute-done | bytes 327712 | tf_op jit(solution)/shard_map/ppermute | solution.py:160
  92.6 2.3 collective-permute-start.19
  94.9 13.2 %collective-permute-done.10 = bf16[320,512]{1,0:T(8,128)(2,1)S(1)} collective-permute-done((bf16[320,512]{1,0:T(8,128)(2,1)}, bf16[320,512]{1,0:T(8,128)(2,1)S(1)}, u32[]{:S(2)}, u32[]{:S(2)}) %collective-permute-start.10) | collective-permute-done | bytes 327712 | tf_op jit(solution)/shard_map/ppermute | solution.py:160
  109.6 7.3 %collective-permute-done.12 = bf16[320,512]{1,0:T(8,128)(2,1)S(1)} collective-permute-done((bf16[320,512]{1,0:T(8,128)(2,1)}, bf16[320,512]{1,0:T(8,128)(2,1)S(1)}, u32[]{:S(2)}, u32[]{:S(2)}) %collective-permute-start.12) | collective-permute-done | bytes 327712 | tf_op jit(solution)/shard_map/ppermute | solution.py:160
  118.4 25.1 %shard_map.111 = (f32[2,128,1600]{2,1,0:T(8,128)}, bf16[8,320,512]{2,1,0:T(8,128)(2,1)}) custom-call(s32[10]{0:T(128)} %pad_add_fusion.4.info_ref, s32[2,1600]{1,0:T(2,128)} %tile.10.rows_ref, bf16[4,1600,128]{2,1,0:T(8,128)(2,1)} %bitcast.119, bf16[4,1600,128]{2,1,0:T(8,128)(2,1)} %bitcast.121, bf16[8,320,512]{2,1,0:T(8,128)(2,1)} %copy-done.6), custom_call_target="tpu_custom_call" | custom-call | flops 20971520000 | bytes 5242880 | tf_op jit(solution)/shard_map/pallas_call | solution.py:118
  143.5 2.8 slice_bitcast_fusion.8
  146.2 14.6 %collective-permute-start.20 = (bf16[320,512]{1,0:T(8,128)(2,1)S(1)}, bf16[320,512]{1,0:T(8,128)(2,1)S(1)}, u32[]{:S(2)}, u32[]{:S(2)}) collective-permute-start(bf16[320,512]{1,0:T(8,128)(2,1)S(1)} %collective-permute-done.13), channel_id=1, source_target_pairs={{0,6},{2,4},{4,2},{6,0},{8,14},{10,12},{12,10},{14,8},{16,22},{18,... | collective-permute-start | bytes 983048 | tf_op jit(solution)/shard_map/ppermute | solution.py:160
  163.4 2.4 collective-permute-start.26
  168.3 25.2 %shard_map.112 = (f32[2,128,1600]{2,1,0:T(8,128)}, bf16[8,320,512]{2,1,0:T(8,128)(2,1)}) custom-call(s32[10]{0:T(128)} %pad_add_fusion.4.info_ref, s32[2,1600]{1,0:T(2,128)} %tile.10.rows_ref, bf16[4,1600,128]{2,1,0:T(8,128)(2,1)} %bitcast.120, bf16[4,1600,128]{2,1,0:T(8,128)(2,1)} %bitcast.122, bf16[8,320,512]{2,1,0:T(8,128)(2,1)} %bitcast_dynamic-update-slice_fusion.kv_ref), custom_call_target="tpu_custom_call" | custom-call | flops 20971520000 | bytes 5242880 | tf_op jit(solution)/shard_map/pallas_call | solution.py:118
  195.9 2.8 slice_bitcast_fusion.2
  198.7 14.4 %collective-permute-start.23 = (bf16[320,512]{1,0:T(8,128)(2,1)}, bf16[320,512]{1,0:T(8,128)(2,1)}, u32[]{:S(2)}, u32[]{:S(2)}) collective-permute-start(bf16[320,512]{1,0:T(8,128)(2,1)} %get-tuple-element.25), channel_id=1, source_target_pairs={{0,6},{2,4},{4,2},{6,0},{8,14},{10,12},{12,10},{14,8},{16,22},{18,... | collective-permute-start | bytes 983048 | tf_op jit(solution)/shard_map/ppermute | solution.py:160
  214.7 2.8 copy.39
  218.0 2.3 collective-permute-start.34
  220.3 2.2 fusion.26
  222.8 2.3 collective-permute-start.31
  225.1 2.1 fusion.11
  227.2 5.6 %collective-permute-done.33 = bf16[320,512]{1,0:T(8,128)(2,1)S(1)} collective-permute-done((bf16[320,512]{1,0:T(8,128)(2,1)S(1)}, bf16[320,512]{1,0:T(8,128)(2,1)S(1)}, u32[]{:S(2)}, u32[]{:S(2)}) %collective-permute-start.33) | collective-permute-done | bytes 327712 | tf_op jit(solution)/shard_map/ppermute | solution.py:160
  240.1 10.2 %collective-permute-done.30 = bf16[320,512]{1,0:T(8,128)(2,1)S(1)} collective-permute-done((bf16[320,512]{1,0:T(8,128)(2,1)}, bf16[320,512]{1,0:T(8,128)(2,1)S(1)}, u32[]{:S(2)}, u32[]{:S(2)}) %collective-permute-start.30) | collective-permute-done | bytes 327712 | tf_op jit(solution)/shard_map/ppermute | solution.py:160
  253.2 18.5 %fusion.29 = f32[320,5120]{1,0:T(8,128)} fusion(bf16[320,2560]{0,1:T(8,128)(2,1)S(1)} %bitcast.111, bf16[5120,2560]{1,0:T(8,128)(2,1)} %param.13), kind=kOutput, calls=%fused_computation.104 | convolution fusion | flops 8388608000 | bytes 34406400 | tf_op jit(solution)/shard_map/dot_general | solution.py:253
  275.5 3.7 %slice_reduce_fusion = (bf16[320,4,128]{2,1,0:T(4,128)(2,1)S(1)}, bf16[320,4,128]{2,1,0:T(4,128)(2,1)S(1)}) fusion(bf16[320,4,2,128]{3,2,1,0:T(2,128)(2,1)S(1)} %reshape.154), kind=kLoop, calls=%fused_computation.38 | loop fusion | bytes 1310720 | tf_op jit(solution)/shard_map/slice | solution.py:245
  279.3 6.6 %convolution_add_fusion.1 = f32[320,5120]{1,0:T(8,128)S(1)} fusion(f32[320,5120]{1,0:T(8,128)} %fusion.29, bf16[320,512]{1,0:T(8,128)(2,1)S(1)} %get-tuple-element.51, bf16[5120,512]{1,0:T(8,128)(2,1)} %param.14), kind=kOutput, calls=%fused_computation.1 | convolution fusion | flops 1679360000 | bytes 18677760 | tf_op jit(solution)/shard_map/dot_general | solution.py:254
  291.2 3.9 %copy.42 = bf16[320,2560]{1,0:T(8,128)(2,1)} copy(bf16[320,2560]{0,1:T(8,128)(2,1)} %bitcast.112) | data formatting | bytes 3276800
  295.1 3.1 %add_convert_fusion = bf16[320,2560]{1,0:T(8,128)(2,1)} fusion(bf16[320,2560]{1,0:T(8,128)(2,1)} %collective-permute-done.37, bf16[320,5120]{1,0:T(8,128)(2,1)S(1)} %fusion, s32[]{:T(128)S(6)} %select_n.163), kind=kLoop, calls=%fused_computation.5 | loop fusion | flops 3276800 | bytes 4915204 | tf_op jit(solution)/shard_map/convert_element_type | solution.py:262
  (136 shorter events, 60.3 us)
Async XLA Ops:
  8.8 48.6 %collective-permute-start.6 = (bf16[320,512]{1,0:T(8,128)(2,1)}, bf16[320,512]{1,0:T(8,128)(2,1)}, u32[]{:S(2)}, u32[]{:S(2)}) collective-permute-start(bf16[320,512]{1,0:T(8,128)(2,1)} %bitcast.110), channel_id=1, source_target_pairs={{0,16},{2,18},{4,20},{6,22},{8,24},{10,26},{12,28},{14,30},{1,17},... | collective-permute-start | bytes 983048 | tf_op jit(solution)/shard_map/ppermute | solution.py:154
  10.1 61.8 %collective-permute-start.5 = (bf16[320,512]{1,0:T(8,128)(2,1)}, bf16[320,512]{1,0:T(8,128)(2,1)}, u32[]{:S(2)}, u32[]{:S(2)}) collective-permute-start(bf16[320,512]{1,0:T(8,128)(2,1)} %bitcast.110), channel_id=1, source_target_pairs={{0,8},{2,10},{4,12},{6,14},{8,16},{10,18},{12,20},{14,22},{16,24},... | collective-permute-start | bytes 983048 | tf_op jit(solution)/shard_map/ppermute | solution.py:154
  11.4 23.8 %collective-permute-start.1 = (s32[1,320]{1,0:T(1,128)S(1)}, s32[1,320]{1,0:T(1,128)S(1)}, u32[]{:S(2)}, u32[]{:S(2)}) collective-permute-start(s32[1,320]{1,0:T(1,128)S(1)} %broadcast_in_dim.35), channel_id=1, source_target_pairs={{0,16},{2,18},{4,20},{6,22},{8,24},{10,26},{12,28},{14,30},{1,17},... | collective-permute-start | bytes 3848 | tf_op jit(solution)/shard_map/ppermute | solution.py:154
  12.7 22.5 %collective-permute-start = (s32[1,320]{1,0:T(1,128)S(1)}, s32[1,320]{1,0:T(1,128)S(1)}, u32[]{:S(2)}, u32[]{:S(2)}) collective-permute-start(s32[1,320]{1,0:T(1,128)S(1)} %broadcast_in_dim.35), channel_id=1, source_target_pairs={{0,8},{2,10},{4,12},{6,14},{8,16},{10,18},{12,20},{14,22},{16,24},... | collective-permute-start | bytes 3848 | tf_op jit(solution)/shard_map/ppermute | solution.py:154
  37.8 15.6 %collective-permute-start.4 = (s32[2,320]{1,0:T(2,128)S(1)}, s32[2,320]{1,0:T(2,128)S(1)}, u32[]{:S(2)}, u32[]{:S(2)}) collective-permute-start(s32[2,320]{1,0:T(2,128)S(1)} %get-tuple-element.47), channel_id=1, source_target_pairs={{0,6},{2,4},{4,2},{6,0},{8,14},{10,12},{12,10},{14,8},{16,22},{18,... | collective-permute-start | bytes 7688 | tf_op jit(solution)/shard_map/ppermute | solution.py:160
  50.5 19.2 %collective-permute-start.14 = (bf16[320,512]{1,0:T(8,128)(2,1)}, bf16[320,512]{1,0:T(8,128)(2,1)S(1)}, u32[]{:S(2)}, u32[]{:S(2)}) collective-permute-start(bf16[320,512]{1,0:T(8,128)(2,1)} %bitcast.125), channel_id=1, source_target_pairs={{0,16},{2,18},{4,20},{6,22},{8,24},{10,26},{12,28},{14,30},{1,17},... | collective-permute-start | bytes 983048 | tf_op jit(solution)/shard_map/ppermute | solution.py:154
  51.8 21.4 %collective-permute-start.13 = (bf16[320,512]{1,0:T(8,128)(2,1)}, bf16[320,512]{1,0:T(8,128)(2,1)S(1)}, u32[]{:S(2)}, u32[]{:S(2)}) collective-permute-start(bf16[320,512]{1,0:T(8,128)(2,1)} %bitcast.126), channel_id=1, source_target_pairs={{0,8},{2,10},{4,12},{6,14},{8,16},{10,18},{12,20},{14,22},{16,24},... | collective-permute-start | bytes 983048 | tf_op jit(solution)/shard_map/ppermute | solution.py:154
  58.4 16.9 %collective-permute-start.7 = (bf16[320,512]{1,0:T(8,128)(2,1)S(1)}, bf16[320,512]{1,0:T(8,128)(2,1)S(1)}, u32[]{:S(2)}, u32[]{:S(2)}) collective-permute-start(bf16[320,512]{1,0:T(8,128)(2,1)S(1)} %get-tuple-element.36), channel_id=1, source_target_pairs={{0,2},{2,0},{4,6},{6,4},{8,10},{10,8},{12,14},{14,12},{16,18},{18,... | collective-permute-start | bytes 983048 | tf_op jit(solution)/shard_map/ppermute | solution.py:160
  59.7 32.9 %collective-permute-start.9 = (bf16[320,512]{1,0:T(8,128)(2,1)S(1)}, bf16[320,512]{1,0:T(8,128)(2,1)S(1)}, u32[]{:S(2)}, u32[]{:S(2)}) collective-permute-start(bf16[320,512]{1,0:T(8,128)(2,1)S(1)} %get-tuple-element.35), channel_id=1, source_target_pairs={{0,4},{2,6},{4,0},{6,2},{8,12},{10,14},{12,8},{14,10},{16,20},{18,... | collective-permute-start | bytes 983048 | tf_op jit(solution)/shard_map/ppermute | solution.py:160
  69.7 38.8 %collective-permute-start.11 = (bf16[320,512]{1,0:T(8,128)(2,1)S(1)}, bf16[320,512]{1,0:T(8,128)(2,1)S(1)}, u32[]{:S(2)}, u32[]{:S(2)}) collective-permute-start(bf16[320,512]{1,0:T(8,128)(2,1)S(1)} %get-tuple-element.34), channel_id=1, source_target_pairs={{0,6},{2,4},{4,2},{6,0},{8,14},{10,12},{12,10},{14,8},{16,22},{18,... | collective-permute-start | bytes 983048 | tf_op jit(solution)/shard_map/ppermute | solution.py:160
  71.9 74.3 %collective-permute-start.15 = (bf16[320,512]{1,0:T(8,128)(2,1)S(1)}, bf16[320,512]{1,0:T(8,128)(2,1)S(1)}, u32[]{:S(2)}, u32[]{:S(2)}) collective-permute-start(bf16[320,512]{1,0:T(8,128)(2,1)S(1)} %get-tuple-element.41), channel_id=1, source_target_pairs={{0,2},{2,0},{4,6},{6,4},{8,10},{10,8},{12,14},{14,12},{16,18},{18,... | collective-permute-start | bytes 983048 | tf_op jit(solution)/shard_map/ppermute | solution.py:160
  73.3 19.1 %collective-permute-start.8 = (bf16[320,512]{1,0:T(8,128)(2,1)}, bf16[320,512]{1,0:T(8,128)(2,1)S(1)}, u32[]{:S(2)}, u32[]{:S(2)}) collective-permute-start(bf16[320,512]{1,0:T(8,128)(2,1)} %collective-permute-done.5), channel_id=1, source_target_pairs={{0,2},{2,0},{4,6},{6,4},{8,10},{10,8},{12,14},{14,12},{16,18},{18,... | collective-permute-start | bytes 983048 | tf_op jit(solution)/shard_map/ppermute | solution.py:160
  75.3 87.0 %collective-permute-start.17 = (bf16[320,512]{1,0:T(8,128)(2,1)S(1)}, bf16[320,512]{1,0:T(8,128)(2,1)S(1)}, u32[]{:S(2)}, u32[]{:S(2)}) collective-permute-start(bf16[320,512]{1,0:T(8,128)(2,1)S(1)} %get-tuple-element.40), channel_id=1, source_target_pairs={{0,4},{2,6},{4,0},{6,2},{8,12},{10,14},{12,8},{14,10},{16,20},{18,... | collective-permute-start | bytes 983048 | tf_op jit(solution)/shard_map/ppermute | solution.py:160
  92.4 15.8 %collective-permute-start.10 = (bf16[320,512]{1,0:T(8,128)(2,1)}, bf16[320,512]{1,0:T(8,128)(2,1)S(1)}, u32[]{:S(2)}, u32[]{:S(2)}) collective-permute-start(bf16[320,512]{1,0:T(8,128)(2,1)} %collective-permute-done.5), channel_id=1, source_target_pairs={{0,4},{2,6},{4,0},{6,2},{8,12},{10,14},{12,8},{14,10},{16,20},{18,... | collective-permute-start | bytes 983048 | tf_op jit(solution)/shard_map/ppermute | solution.py:160
  92.6 73.9 %collective-permute-start.19 = (bf16[320,512]{1,0:T(8,128)(2,1)S(1)}, bf16[320,512]{1,0:T(8,128)(2,1)S(1)}, u32[]{:S(2)}, u32[]{:S(2)}) collective-permute-start(bf16[320,512]{1,0:T(8,128)(2,1)S(1)} %get-tuple-element.39), channel_id=1, source_target_pairs={{0,6},{2,4},{4,2},{6,0},{8,14},{10,12},{12,10},{14,8},{16,22},{18,... | collective-permute-start | bytes 983048 | tf_op jit(solution)/shard_map/ppermute | solution.py:160
  108.6 53.0 %collective-permute-start.16 = (bf16[320,512]{1,0:T(8,128)(2,1)S(1)}, bf16[320,512]{1,0:T(8,128)(2,1)S(1)}, u32[]{:S(2)}, u32[]{:S(2)}) collective-permute-start(bf16[320,512]{1,0:T(8,128)(2,1)S(1)} %collective-permute-done.13), channel_id=1, source_target_pairs={{0,2},{2,0},{4,6},{6,4},{8,10},{10,8},{12,14},{14,12},{16,18},{18,... | collective-permute-start | bytes 983048 | tf_op jit(solution)/shard_map/ppermute | solution.py:160
  116.9 46.5 %collective-permute-start.18 = (bf16[320,512]{1,0:T(8,128)(2,1)S(1)}, bf16[320,512]{1,0:T(8,128)(2,1)S(1)}, u32[]{:S(2)}, u32[]{:S(2)}) collective-permute-start(bf16[320,512]{1,0:T(8,128)(2,1)S(1)} %collective-permute-done.13), channel_id=1, source_target_pairs={{0,4},{2,6},{4,0},{6,2},{8,12},{10,14},{12,8},{14,10},{16,20},{18,... | collective-permute-start | bytes 983048 | tf_op jit(solution)/shard_map/ppermute | solution.py:160
  146.2 21.0 %collective-permute-start.20 = (bf16[320,512]{1,0:T(8,128)(2,1)S(1)}, bf16[320,512]{1,0:T(8,128)(2,1)S(1)}, u32[]{:S(2)}, u32[]{:S(2)}) collective-permute-start(bf16[320,512]{1,0:T(8,128)(2,1)S(1)} %collective-permute-done.13), channel_id=1, source_target_pairs={{0,6},{2,4},{4,2},{6,0},{8,14},{10,12},{12,10},{14,8},{16,22},{18,... | collective-permute-start | bytes 983048 | tf_op jit(solution)/shard_map/ppermute | solution.py:160
  161.6 37.1 %collective-permute-start.24 = (bf16[320,512]{1,0:T(8,128)(2,1)}, bf16[320,512]{1,0:T(8,128)(2,1)}, u32[]{:S(2)}, u32[]{:S(2)}) collective-permute-start(bf16[320,512]{1,0:T(8,128)(2,1)} %get-tuple-element.22), channel_id=1, source_target_pairs={{0,2},{2,0},{4,6},{6,4},{8,10},{10,8},{12,14},{14,12},{16,18},{18,... | collective-permute-start | bytes 983048 | tf_op jit(solution)/shard_map/ppermute | solution.py:160
  162.3 50.8 %collective-permute-start.25 = (bf16[320,512]{1,0:T(8,128)(2,1)}, bf16[320,512]{1,0:T(8,128)(2,1)}, u32[]{:S(2)}, u32[]{:S(2)}) collective-permute-start(bf16[320,512]{1,0:T(8,128)(2,1)} %get-tuple-element.24), channel_id=1, source_target_pairs={{0,4},{2,6},{4,0},{6,2},{8,12},{10,14},{12,8},{14,10},{16,20},{18,... | collective-permute-start | bytes 983048 | tf_op jit(solution)/shard_map/ppermute | solution.py:160
  163.4 54.1 %collective-permute-start.26 = (bf16[320,512]{1,0:T(8,128)(2,1)}, bf16[320,512]{1,0:T(8,128)(2,1)}, u32[]{:S(2)}, u32[]{:S(2)}) collective-permute-start(bf16[320,512]{1,0:T(8,128)(2,1)} %get-tuple-element.23), channel_id=1, source_target_pairs={{0,6},{2,4},{4,2},{6,0},{8,14},{10,12},{12,10},{14,8},{16,22},{18,... | collective-permute-start | bytes 983048 | tf_op jit(solution)/shard_map/ppermute | solution.py:160
  166.5 51.5 %collective-permute-start.21 = (bf16[320,512]{1,0:T(8,128)(2,1)}, bf16[320,512]{1,0:T(8,128)(2,1)}, u32[]{:S(2)}, u32[]{:S(2)}) collective-permute-start(bf16[320,512]{1,0:T(8,128)(2,1)} %get-tuple-element.27), channel_id=1, source_target_pairs={{0,2},{2,0},{4,6},{6,4},{8,10},{10,8},{12,14},{14,12},{16,18},{18,... | collective-permute-start | bytes 983048 | tf_op jit(solution)/shard_map/ppermute | solution.py:160
  167.3 55.2 %collective-permute-start.22 = (bf16[320,512]{1,0:T(8,128)(2,1)}, bf16[320,512]{1,0:T(8,128)(2,1)}, u32[]{:S(2)}, u32[]{:S(2)}) collective-permute-start(bf16[320,512]{1,0:T(8,128)(2,1)} %get-tuple-element.26), channel_id=1, source_target_pairs={{0,4},{2,6},{4,0},{6,2},{8,12},{10,14},{12,8},{14,10},{16,20},{18,... | collective-permute-start | bytes 983048 | tf_op jit(solution)/shard_map/ppermute | solution.py:160
  198.7 23.7 %collective-permute-start.23 = (bf16[320,512]{1,0:T(8,128)(2,1)}, bf16[320,512]{1,0:T(8,128)(2,1)}, u32[]{:S(2)}, u32[]{:S(2)}) collective-permute-start(bf16[320,512]{1,0:T(8,128)(2,1)} %get-tuple-element.25), channel_id=1, source_target_pairs={{0,6},{2,4},{4,2},{6,0},{8,14},{10,12},{12,10},{14,8},{16,22},{18,... | collective-permute-start | bytes 983048 | tf_op jit(solution)/shard_map/ppermute | solution.py:160
  218.0 16.0 %collective-permute-start.34 = (bf16[320,512]{1,0:T(8,128)(2,1)}, bf16[320,512]{1,0:T(8,128)(2,1)S(1)}, u32[]{:S(2)}, u32[]{:S(2)}) collective-permute-start(bf16[320,512]{1,0:T(8,128)(2,1)} %get-tuple-element.29), channel_id=1, source_target_pairs={{0,6},{2,4},{4,2},{6,0},{8,14},{10,12},{12,10},{14,8},{16,22},{18,... | collective-permute-start | bytes 983048 | tf_op jit(solution)/shard_map/ppermute | solution.py:160
  222.4 15.6 %collective-permute-start.29 = (bf16[320,512]{1,0:T(8,128)(2,1)}, bf16[320,512]{1,0:T(8,128)(2,1)S(1)}, u32[]{:S(2)}, u32[]{:S(2)}) collective-permute-start(bf16[320,512]{1,0:T(8,128)(2,1)} %get-tuple-element.33), channel_id=1, source_target_pairs={{0,2},{2,0},{4,6},{6,4},{8,10},{10,8},{12,14},{14,12},{16,18},{18,... | collective-permute-start | bytes 983048 | tf_op jit(solution)/shard_map/ppermute | solution.py:160
  222.4 27.8 %collective-permute-start.30 = (bf16[320,512]{1,0:T(8,128)(2,1)}, bf16[320,512]{1,0:T(8,128)(2,1)S(1)}, u32[]{:S(2)}, u32[]{:S(2)}) collective-permute-start(bf16[320,512]{1,0:T(8,128)(2,1)} %get-tuple-element.32), channel_id=1, source_target_pairs={{0,4},{2,6},{4,0},{6,2},{8,12},{10,14},{12,8},{14,10},{16,20},{18,... | collective-permute-start | bytes 983048 | tf_op jit(solution)/shard_map/ppermute | solution.py:160
  222.8 27.5 %collective-permute-start.31 = (bf16[320,512]{1,0:T(8,128)(2,1)}, bf16[320,512]{1,0:T(8,128)(2,1)S(1)}, u32[]{:S(2)}, u32[]{:S(2)}) collective-permute-start(bf16[320,512]{1,0:T(8,128)(2,1)} %get-tuple-element.31), channel_id=1, source_target_pairs={{0,6},{2,4},{4,2},{6,0},{8,14},{10,12},{12,10},{14,8},{16,22},{18,... | collective-permute-start | bytes 983048 | tf_op jit(solution)/shard_map/ppermute | solution.py:160
  232.7 39.0 %collective-permute-start.27 = (bf16[320,512]{1,0:T(8,128)(2,1)}, bf16[320,512]{1,0:T(8,128)(2,1)S(1)}, u32[]{:S(2)}, u32[]{:S(2)}) collective-permute-start(bf16[320,512]{1,0:T(8,128)(2,1)} %fusion.26), channel_id=1, source_target_pairs={{8,0},{10,2},{12,4},{14,6},{16,8},{18,10},{20,12},{22,14},{24,16},... | collective-permute-start | bytes 983048 | tf_op jit(solution)/shard_map/ppermute | solution.py:154
  234.0 37.7 %collective-permute-start.28 = (bf16[320,512]{1,0:T(8,128)(2,1)}, bf16[320,512]{1,0:T(8,128)(2,1)}, u32[]{:S(2)}, u32[]{:S(2)}) collective-permute-start(bf16[320,512]{1,0:T(8,128)(2,1)} %fusion.11), channel_id=1, source_target_pairs={{16,0},{18,2},{20,4},{22,6},{24,8},{26,10},{28,12},{30,14},{17,1},... | collective-permute-start | bytes 983048 | tf_op jit(solution)/shard_map/ppermute | solution.py:154
  238.0 35.4 %collective-permute-start.35 = (bf16[320,512]{1,0:T(8,128)(2,1)}, bf16[320,512]{1,0:T(8,128)(2,1)}, u32[]{:S(2)}, u32[]{:S(2)}) collective-permute-start(bf16[320,512]{1,0:T(8,128)(2,1)} %fusion.23), channel_id=1, source_target_pairs={{8,0},{10,2},{12,4},{14,6},{16,8},{18,10},{20,12},{22,14},{24,16},... | collective-permute-start | bytes 983048 | tf_op jit(solution)/shard_map/ppermute | solution.py:154
  251.2 22.2 %collective-permute-start.36 = (bf16[320,512]{1,0:T(8,128)(2,1)}, bf16[320,512]{1,0:T(8,128)(2,1)}, u32[]{:S(2)}, u32[]{:S(2)}) collective-permute-start(bf16[320,512]{1,0:T(8,128)(2,1)} %fusion.20), channel_id=1, source_target_pairs={{16,0},{18,2},{20,4},{22,6},{24,8},{26,10},{28,12},{30,14},{17,1},... | collective-permute-start | bytes 983048 | tf_op jit(solution)/shard_map/ppermute | solution.py:154
  (16 other events, 206.1 us)

commit v3 on v2

--- a/solution.py
+++ b/solution.py
@@ -160,6 +160,11 @@
     return lax.ppermute(block, "dc", [(i, i ^ mask) for i in range(lax.axis_size("dc"))])
 
 
+def after(block, *arrived):
+    wait = sum(x.reshape(-1)[0] * 0 for x in arrived)
+    return block + wait
+
+
 def shards(
     queries,
     keys,
@@ -184,15 +189,21 @@
         axis=2,
     ).reshape(tok, chunks, -1)
     windows = []
+    near = far = slots = None
     for c in range(chunks):
         own = pairs[:, c]
+        if c:
+            own = after(own, near, far)
         near = shift(own, PLANE)
         far = shift(own, 2 * PLANE)
-        slots = [own, near]
+        send_near, send_far = near, far
+        if c:
+            send_near, send_far = (after(x, *slots[2:]) for x in (near, far))
+        slots = [own[None], near[None]]
         for mask in range(1, PLANE):
-            slots.append(swap(jnp.where(lane < (lane ^ mask), own, far), mask))
-            slots.append(swap(near, mask))
-        windows.append(jnp.stack(slots))
+            first = jnp.where(lane < (lane ^ mask), own, send_far)
+            slots.append(swap(jnp.stack([first, send_near]), mask))
+        windows.append(jnp.concatenate(slots))
 
     bases = [me, me - PLANE]
     for mask in range(1, PLANE):
@@ -232,8 +243,9 @@
         near = parts[1].astype(f32)
         far = jnp.zeros_like(near)
         for mask in range(1, PLANE):
-            back = swap(parts[2 * mask], mask).astype(f32)
-            near = near + swap(parts[2 * mask + 1], mask).astype(f32)
+            got = swap(parts[2 * mask : 2 * mask + 2], mask).astype(f32)
+            back = got[0]
+            near = near + got[1]
             ahead = lane < (lane ^ mask)
             own = own + jnp.where(ahead, back, 0.0)
             far = far + jnp.where(ahead, 0.0, back)

time: 299 us -> 256 us (0.86)
  waiting for transfers between devices: 81.4 us -> 33.8 us
  starting transfers between devices: 67.7 us -> 55.6 us
  other arithmetic: 20.3 us -> 27.6 us
  local copies, waits for them, and re-layouts: 50.3 us -> 53.7 us
  between operations: 1.14 us -> 4.53 us
    ppermute x27 -> x15, waiting for transfers between devices: 53.1 us -> 24.9 us  [swap(): lax.ppermute(block, 'dc', [(i, i ^ mask) for i in range(lax.axis_size('dc...]
    ppermute x10, waiting for transfers between devices: 28.3 us -> 8.92 us  [shift(): lax.ppermute(block, 'dc', [(i, i + distance) for i in devices if i + dist...]
    ppermute x27 -> x15, starting transfers between devices: 50.4 us -> 36.1 us  [swap(): lax.ppermute(block, 'dc', [(i, i ^ mask) for i in range(lax.axis_size('dc...]
    slice x0 -> x7, local copies, waits for them, and re-layouts: none -> 8.3 us  [the longest x2 5.57 us: shards(): got = swap(parts[2 * mask:2 * mask + 2], mask).astype(f32)]
    squeeze x2 -> x0, local copies, waits for them, and re-layouts: 5.51 us -> none  [shards(): near = near + swap(parts[2 * mask + 1], mask).astype(f32)]
    add x0 -> x3, other arithmetic: none -> 4.35 us  [the longest x2 4.3 us: shards(): near = near + got[1]]
    unnamed x39 -> x40, local copies, waits for them, and re-layouts: 21.3 us -> 20.1 us
    convert_element_type x4 -> x6, other arithmetic: 7.11 us -> 7.94 us  [shards(): got = swap(parts[2 * mask:2 * mask + 2], mask).astype(f32)]
  transfers between devices with their start and end apart: 38 -> 26, of which waited for: 7 -> 4; matrix products, arithmetic and copies ran while one was open for 23% -> 33% of each run, Pallas kernels for 17% -> 20%
where the time goes in v3:
time: 256 us; the launch traced here: 254 us
  starting transfers between devices  55.6 us (22%)
  local copies, waits for them, and re-layouts  53.7 us (21%)
  Pallas kernels  50.3 us (20%)
  waiting for transfers between devices  33.8 us (13%)
  matrix products  29 us (11%)
  other arithmetic  27.6 us (11%)
  between operations  4.53 us (2%)
    pallas_call x2, Pallas kernels, attention(): pl.pallas_call(attention_kernel, grid=(heads,), in_specs=[pl.BlockSpec(me...  50.3 us
    ppermute x15, starting transfers between devices, swap(): lax.ppermute(block, 'dc', [(i, i ^ mask) for i in range(lax.axis_size('dc...  36.1 us
    ppermute x15, waiting for transfers between devices, swap(): lax.ppermute(block, 'dc', [(i, i ^ mask) for i in range(lax.axis_size('dc...  24.9 us
    unnamed x40, local copies, waits for them, and re-layouts  20.1 us
    dot_general x1, matrix products, shards(): term = dot(query_grad, w_query)  18 us
    ppermute x10, starting transfers between devices, shift(): lax.ppermute(block, 'dc', [(i, i + distance) for i in devices if i + dist...  16 us
    ppermute x10, waiting for transfers between devices, shift(): lax.ppermute(block, 'dc', [(i, i + distance) for i in devices if i + dist...  8.92 us
    convert_element_type x6, other arithmetic, shards(): got = swap(parts[2 * mask:2 * mask + 2], mask).astype(f32)  7.94 us
  transfers between devices with their start and end apart: 26, of which 4 were waited for; matrix products, arithmetic and copies ran while one was open for 33% of the time, Pallas kernels for 20%

profile of v3, /device:TPU:25, one launch (start us, length us, event | category | flops | bytes accessed | tf_op | source)
XLA Modules:
  0.0 254.5 jit_solution(16666166259193147432)
XLA Ops:
  3.9 2.4 reshape.257
  6.3 2.4 reshape.258
  15.7 2.2 collective-permute-start.4
  18.4 3.6 %copy.29 = bf16[320,2560]{0,1:T(8,128)(2,1)S(1)} copy(bf16[320,2560]{1,0:T(8,128)(2,1)} %param.8) | data formatting | bytes 3276800 | tf_op args[0]
  22.0 2.3 copy.30
  24.3 3.6 %copy.31 = bf16[320,2560]{0,1:T(8,128)(2,1)S(1)} copy(bf16[320,2560]{1,0:T(8,128)(2,1)} %param.11) | data formatting | bytes 3276800 | tf_op args[3]
  27.9 2.3 copy.32
  44.0 2.2 collective-permute-start.9
  47.8 8.9 %collective-permute-done.10 = bf16[320,512]{1,0:T(8,128)(2,1)S(1)} collective-permute-done((bf16[320,512]{1,0:T(8,128)(2,1)S(1)}, bf16[320,512]{1,0:T(8,128)(2,1)S(1)}, u32[]{:S(2)}, u32[]{:S(2)}) %collective-permute-start.10) | collective-permute-done | bytes 327712 | tf_op jit(solution)/shard_map/ppermute | solution.py:154
  56.7 3.0 %collective-permute-done.9 = bf16[2,320,512]{2,1,0:T(8,128)(2,1)S(1)} collective-permute-done((bf16[2,320,512]{2,1,0:T(8,128)(2,1)S(1)}, bf16[2,320,512]{2,1,0:T(8,128)(2,1)S(1)}, u32[]{:S(2)}, u32[]{:S(2)}) %collective-permute-start.9) | collective-permute-done | bytes 655392 | tf_op jit(solution)/shard_map/ppermute | solution.py:160
  60.6 15.1 %collective-permute-done.8 = bf16[2,320,512]{2,1,0:T(8,128)(2,1)S(1)} collective-permute-done((bf16[2,320,512]{2,1,0:T(8,128)(2,1)S(1)}, bf16[2,320,512]{2,1,0:T(8,128)(2,1)S(1)}, u32[]{:S(2)}, u32[]{:S(2)}) %collective-permute-start.8) | collective-permute-done | bytes 655392 | tf_op jit(solution)/shard_map/ppermute | solution.py:160
  83.8 25.2 %shard_map.111 = (f32[2,128,1600]{2,1,0:T(8,128)}, bf16[8,320,512]{2,1,0:T(8,128)(2,1)}) custom-call(s32[10]{0:T(128)} %pad_add_fusion.4.info_ref, s32[2,1600]{1,0:T(2,128)} %tile.10.rows_ref, bf16[4,1600,128]{2,1,0:T(8,128)(2,1)} %bitcast.105, bf16[4,1600,128]{2,1,0:T(8,128)(2,1)} %bitcast.107, bf16[8,320,512]{2,1,0:T(8,128)(2,1)} %copy-done.10), custom_call_target="tpu_custom_call" | custom-call | flops 20971520000 | bytes 5242880 | tf_op jit(solution)/shard_map/pallas_call | solution.py:118
  109.0 2.8 %fusion.14 = (bf16[2,320,512]{2,1,0:T(8,128)(2,1)S(1)}, bf16[2,320,512]{2,1,0:T(8,128)(2,1)}, bf16[2,320,512]{2,1,0:T(8,128)(2,1)}) fusion(bf16[8,320,512]{2,1,0:T(8,128)(2,1)} %get-tuple-element.10), kind=kLoop, calls=%fused_computation.74 | loop fusion | bytes 3932160 | tf_op jit(solution)/shard_map/slice | solution.py:246
  111.8 5.2 %collective-permute-start.15 = (bf16[2,320,512]{2,1,0:T(8,128)(2,1)S(1)}, bf16[2,320,512]{2,1,0:T(8,128)(2,1)}, u32[]{:S(2)}, u32[]{:S(2)}) collective-permute-start(bf16[2,320,512]{2,1,0:T(8,128)(2,1)S(1)} %get-tuple-element.26), channel_id=1, source_target_pairs={{0,2},{2,0},{4,6},{6,4},{8,10},{10,8},{12,14},{14,12},{16,18},{18,... | collective-permute-start | bytes 1966088 | tf_op jit(solution)/shard_map/ppermute | solution.py:160
  117.0 7.8 %collective-permute-start.17 = (bf16[2,320,512]{2,1,0:T(8,128)(2,1)}, bf16[2,320,512]{2,1,0:T(8,128)(2,1)}, u32[]{:S(2)}, u32[]{:S(2)}) collective-permute-start(bf16[2,320,512]{2,1,0:T(8,128)(2,1)} %get-tuple-element.27), channel_id=1, source_target_pairs={{0,6},{2,4},{4,2},{6,0},{8,14},{10,12},{12,10},{14,8},{16,22},{18,... | collective-permute-start | bytes 1966088 | tf_op jit(solution)/shard_map/ppermute | solution.py:160
  126.7 25.1 %shard_map.112 = (f32[2,128,1600]{2,1,0:T(8,128)}, bf16[8,320,512]{2,1,0:T(8,128)(2,1)}) custom-call(s32[10]{0:T(128)} %pad_add_fusion.4.info_ref, s32[2,1600]{1,0:T(2,128)} %tile.10.rows_ref, bf16[4,1600,128]{2,1,0:T(8,128)(2,1)} %bitcast.106, bf16[4,1600,128]{2,1,0:T(8,128)(2,1)} %bitcast.108, bf16[8,320,512]{2,1,0:T(8,128)(2,1)} %copy-done.8), custom_call_target="tpu_custom_call" | custom-call | flops 20971520000 | bytes 5242880 | tf_op jit(solution)/shard_map/pallas_call | solution.py:118
  151.8 2.8 %fusion.15 = (bf16[2,320,512]{2,1,0:T(8,128)(2,1)}, bf16[2,320,512]{2,1,0:T(8,128)(2,1)}, bf16[2,320,512]{2,1,0:T(8,128)(2,1)}) fusion(bf16[8,320,512]{2,1,0:T(8,128)(2,1)} %get-tuple-element.11), kind=kLoop, calls=%fused_computation.75 | loop fusion | bytes 3932160 | tf_op jit(solution)/shard_map/slice | solution.py:246
  154.6 5.2 %collective-permute-start.20 = (bf16[2,320,512]{2,1,0:T(8,128)(2,1)}, bf16[2,320,512]{2,1,0:T(8,128)(2,1)}, u32[]{:S(2)}, u32[]{:S(2)}) collective-permute-start(bf16[2,320,512]{2,1,0:T(8,128)(2,1)} %get-tuple-element.29), channel_id=1, source_target_pairs={{0,2},{2,0},{4,6},{6,4},{8,10},{10,8},{12,14},{14,12},{16,18},{18,... | collective-permute-start | bytes 1966088 | tf_op jit(solution)/shard_map/ppermute | solution.py:160
  159.8 9.2 %collective-permute-start.22 = (bf16[2,320,512]{2,1,0:T(8,128)(2,1)}, bf16[2,320,512]{2,1,0:T(8,128)(2,1)}, u32[]{:S(2)}, u32[]{:S(2)}) collective-permute-start(bf16[2,320,512]{2,1,0:T(8,128)(2,1)} %get-tuple-element.30), channel_id=1, source_target_pairs={{0,6},{2,4},{4,2},{6,0},{8,14},{10,12},{12,10},{14,8},{16,22},{18,... | collective-permute-start | bytes 1966088 | tf_op jit(solution)/shard_map/ppermute | solution.py:160
  171.0 2.6 %copy.38 = f32[2,128,1600]{1,2,0:T(8,128)} copy(f32[2,128,1600]{2,1,0:T(8,128)} %get-tuple-element.9) | data formatting | bytes 3276800 | tf_op jit(solution)/shard_map/pallas_call | solution.py:118
  175.5 2.6 %copy.39 = bf16[320,4,5,128]{0,3,2,1:T(8,128)(2,1)} copy(bf16[320,4,5,128]{3,0,2,1:T(8,128)(2,1)S(1)} %fusion.2) | data formatting | bytes 3276800 | tf_op jit(solution)/shard_map/transpose | solution.py:260
  189.0 6.8 %collective-permute-done.22 = bf16[2,320,512]{2,1,0:T(8,128)(2,1)} collective-permute-done((bf16[2,320,512]{2,1,0:T(8,128)(2,1)}, bf16[2,320,512]{2,1,0:T(8,128)(2,1)}, u32[]{:S(2)}, u32[]{:S(2)}) %collective-permute-start.22) | collective-permute-done | bytes 655392 | tf_op jit(solution)/shard_map/ppermute | solution.py:160
  198.8 2.6 %fusion.12 = (bf16[320,512]{1,0:T(8,128)(2,1)}, bf16[320,512]{1,0:T(8,128)(2,1)}) fusion(f32[2,320,512]{2,1,0:T(8,128)S(1)} %convert_element_type.100, f32[2,320,512]{2,1,0:T(8,128)S(1)} %convert_element_type.99, f32[2,320,512]{2,1,0:T(8,128)S(1)} %convert_element_type.98, bf16[8,320,512]{2,1,0:T(8,128)(2,1)} %get-tuple-element.11, pred[]{:T(512)S(6)} %lt.63, ...), kind=kLoop, calls=%fused_computation.37 | loop fusion | flops 1802240 | bytes 4915203 | tf_op jit(solution)/shard_map/add | solution.py:248
  201.4 2.0 collective-permute-start.23
  203.4 2.0 collective-permute-start.24
  205.5 18.0 %fusion.18 = f32[320,5120]{1,0:T(8,128)} fusion(bf16[320,2560]{0,1:T(8,128)(2,1)} %bitcast.96, bf16[5120,2560]{1,0:T(8,128)(2,1)} %param.13), kind=kOutput, calls=%fused_computation.78 | convolution fusion | flops 8388608000 | bytes 34406400 | tf_op jit(solution)/shard_map/dot_general | solution.py:265
  227.9 3.7 %slice_reduce_fusion = (bf16[320,4,128]{2,1,0:T(4,128)(2,1)S(1)}, bf16[320,4,128]{2,1,0:T(4,128)(2,1)S(1)}) fusion(bf16[320,4,2,128]{3,2,1,0:T(2,128)(2,1)S(1)} %reshape.256), kind=kLoop, calls=%fused_computation.14 | loop fusion | bytes 1310720 | tf_op jit(solution)/shard_map/slice | solution.py:257
  231.7 6.5 %convolution_add_fusion.1 = f32[320,5120]{1,0:T(8,128)S(1)} fusion(f32[320,5120]{1,0:T(8,128)} %fusion.18, bf16[320,512]{1,0:T(8,128)(2,1)S(1)} %get-tuple-element.55, bf16[5120,512]{1,0:T(8,128)(2,1)} %param.14), kind=kOutput, calls=%fused_computation.1 | convolution fusion | flops 1679360000 | bytes 18677760 | tf_op jit(solution)/shard_map/dot_general | solution.py:266
  238.3 4.5 %fusion = bf16[320,5120]{1,0:T(8,128)(2,1)S(1)} fusion(f32[320,5120]{1,0:T(8,128)S(1)} %convolution_add_fusion.1, bf16[320,512]{1,0:T(8,128)(2,1)S(1)} %get-tuple-element.54, bf16[5120,512]{1,0:T(8,128)(2,1)} %param.15), kind=kOutput, calls=%fused_computation.2 | convolution fusion | flops 1680998400 | bytes 15400960 | tf_op jit(solution)/shard_map/dot_general | solution.py:266
  244.1 3.4 %collective-permute-start.25 = (bf16[320,2560]{1,0:T(8,128)(2,1)}, bf16[320,2560]{1,0:T(8,128)(2,1)}, u32[]{:S(2)}, u32[]{:S(2)}) collective-permute-start(bf16[320,2560]{1,0:T(8,128)(2,1)} %constant_dynamic-slice_fusion), channel_id=1, source_target_pairs={{0,1},{1,0},{2,3},{3,2},{4,5},{5,4},{6,7},{7,6},{8,9},{9,8},{10,11... | collective-permute-start | bytes 4915208 | tf_op jit(solution)/shard_map/ppermute | solution.py:273
  247.5 3.9 %copy.42 = bf16[320,2560]{1,0:T(8,128)(2,1)} copy(bf16[320,2560]{0,1:T(8,128)(2,1)} %bitcast.97) | data formatting | bytes 3276800
  251.4 3.1 %add_convert_fusion = bf16[320,2560]{1,0:T(8,128)(2,1)} fusion(bf16[320,2560]{1,0:T(8,128)(2,1)} %collective-permute-done.25, bf16[320,5120]{1,0:T(8,128)(2,1)S(1)} %fusion, s32[]{:T(128)S(6)} %select_n.184), kind=kLoop, calls=%fused_computation.5 | loop fusion | flops 3276800 | bytes 4915204 | tf_op jit(solution)/shard_map/convert_element_type | solution.py:274
  (126 shorter events, 56.9 us)
Async XLA Ops:
  1.3 14.3 %collective-permute-start.1 = (s32[1,320]{1,0:T(1,128)S(1)}, s32[1,320]{1,0:T(1,128)S(1)}, u32[]{:S(2)}, u32[]{:S(2)}) collective-permute-start(s32[1,320]{1,0:T(1,128)S(1)} %broadcast_in_dim.42), channel_id=1, source_target_pairs={{0,16},{2,18},{4,20},{6,22},{8,24},{10,26},{12,28},{14,30},{1,17},... | collective-permute-start | bytes 3848 | tf_op jit(solution)/shard_map/ppermute | solution.py:154
  2.6 13.0 %collective-permute-start = (s32[1,320]{1,0:T(1,128)S(1)}, s32[1,320]{1,0:T(1,128)S(1)}, u32[]{:S(2)}, u32[]{:S(2)}) collective-permute-start(s32[1,320]{1,0:T(1,128)S(1)} %broadcast_in_dim.42), channel_id=1, source_target_pairs={{0,8},{2,10},{4,12},{6,14},{8,16},{10,18},{12,20},{14,22},{16,24},... | collective-permute-start | bytes 3848 | tf_op jit(solution)/shard_map/ppermute | solution.py:154
  10.4 5.2 %copy-start.11 = (s32[320]{0:T(512)S(1)}, s32[320]{0:T(512)}, u32[]{:S(2)}) copy-start(s32[320]{0:T(512)} %param.12) | copy-start | bytes 3844
  12.1 22.1 %collective-permute-start.6 = (bf16[320,512]{1,0:T(8,128)(2,1)}, bf16[320,512]{1,0:T(8,128)(2,1)}, u32[]{:S(2)}, u32[]{:S(2)}) collective-permute-start(bf16[320,512]{1,0:T(8,128)(2,1)} %bitcast.95), channel_id=1, source_target_pairs={{0,16},{2,18},{4,20},{6,22},{8,24},{10,26},{12,28},{14,30},{1,17},... | collective-permute-start | bytes 983048 | tf_op jit(solution)/shard_map/ppermute | solution.py:154
  13.4 22.5 %collective-permute-start.5 = (bf16[320,512]{1,0:T(8,128)(2,1)}, bf16[320,512]{1,0:T(8,128)(2,1)}, u32[]{:S(2)}, u32[]{:S(2)}) collective-permute-start(bf16[320,512]{1,0:T(8,128)(2,1)} %bitcast.95), channel_id=1, source_target_pairs={{0,8},{2,10},{4,12},{6,14},{8,16},{10,18},{12,20},{14,22},{16,24},... | collective-permute-start | bytes 983048 | tf_op jit(solution)/shard_map/ppermute | solution.py:154
  15.7 14.5 %collective-permute-start.4 = (s32[2,320]{1,0:T(2,128)S(1)}, s32[2,320]{1,0:T(2,128)S(1)}, u32[]{:S(2)}, u32[]{:S(2)}) collective-permute-start(s32[2,320]{1,0:T(2,128)S(1)} %get-tuple-element.51), channel_id=1, source_target_pairs={{0,6},{2,4},{4,2},{6,0},{8,14},{10,12},{12,10},{14,8},{16,22},{18,... | collective-permute-start | bytes 7688 | tf_op jit(solution)/shard_map/ppermute | solution.py:160
  17.9 12.3 %collective-permute-start.3 = (s32[2,320]{1,0:T(2,128)S(1)}, s32[2,320]{1,0:T(2,128)S(1)}, u32[]{:S(2)}, u32[]{:S(2)}) collective-permute-start(s32[2,320]{1,0:T(2,128)S(1)} %get-tuple-element.52), channel_id=1, source_target_pairs={{0,4},{2,6},{4,0},{6,2},{8,12},{10,14},{12,8},{14,10},{16,20},{18,... | collective-permute-start | bytes 7688 | tf_op jit(solution)/shard_map/ppermute | solution.py:160
  18.1 12.1 %collective-permute-start.2 = (s32[2,320]{1,0:T(2,128)S(1)}, s32[2,320]{1,0:T(2,128)S(1)}, u32[]{:S(2)}, u32[]{:S(2)}) collective-permute-start(s32[2,320]{1,0:T(2,128)S(1)} %get-tuple-element.53), channel_id=1, source_target_pairs={{0,2},{2,0},{4,6},{6,4},{8,10},{10,8},{12,14},{14,12},{16,18},{18,... | collective-permute-start | bytes 7688 | tf_op jit(solution)/shard_map/ppermute | solution.py:160
  38.9 40.3 %collective-permute-start.11 = (bf16[320,512]{1,0:T(8,128)(2,1)S(1)}, bf16[320,512]{1,0:T(8,128)(2,1)S(1)}, u32[]{:S(2)}, u32[]{:S(2)}) collective-permute-start(bf16[320,512]{1,0:T(8,128)(2,1)S(1)} %fusion.13), channel_id=1, source_target_pairs={{0,16},{2,18},{4,20},{6,22},{8,24},{10,26},{12,28},{14,30},{1,17},... | collective-permute-start | bytes 983048 | tf_op jit(solution)/shard_map/ppermute | solution.py:154
  40.2 16.5 %collective-permute-start.10 = (bf16[320,512]{1,0:T(8,128)(2,1)S(1)}, bf16[320,512]{1,0:T(8,128)(2,1)S(1)}, u32[]{:S(2)}, u32[]{:S(2)}) collective-permute-start(bf16[320,512]{1,0:T(8,128)(2,1)S(1)} %fusion.13), channel_id=1, source_target_pairs={{0,8},{2,10},{4,12},{6,14},{8,16},{10,18},{12,20},{14,22},{16,24},... | collective-permute-start | bytes 983048 | tf_op jit(solution)/shard_map/ppermute | solution.py:154
  44.0 15.7 %collective-permute-start.9 = (bf16[2,320,512]{2,1,0:T(8,128)(2,1)S(1)}, bf16[2,320,512]{2,1,0:T(8,128)(2,1)S(1)}, u32[]{:S(2)}, u32[]{:S(2)}) collective-permute-start(bf16[2,320,512]{2,1,0:T(8,128)(2,1)S(1)} %get-tuple-element.43), channel_id=1, source_target_pairs={{0,6},{2,4},{4,2},{6,0},{8,14},{10,12},{12,10},{14,8},{16,22},{18,... | collective-permute-start | bytes 1966088 | tf_op jit(solution)/shard_map/ppermute | solution.py:160
  46.2 29.4 %collective-permute-start.8 = (bf16[2,320,512]{2,1,0:T(8,128)(2,1)S(1)}, bf16[2,320,512]{2,1,0:T(8,128)(2,1)S(1)}, u32[]{:S(2)}, u32[]{:S(2)}) collective-permute-start(bf16[2,320,512]{2,1,0:T(8,128)(2,1)S(1)} %get-tuple-element.44), channel_id=1, source_target_pairs={{0,4},{2,6},{4,0},{6,2},{8,12},{10,14},{12,8},{14,10},{16,20},{18,... | collective-permute-start | bytes 1966088 | tf_op jit(solution)/shard_map/ppermute | solution.py:160
  46.5 30.0 %collective-permute-start.7 = (bf16[2,320,512]{2,1,0:T(8,128)(2,1)S(1)}, bf16[2,320,512]{2,1,0:T(8,128)(2,1)S(1)}, u32[]{:S(2)}, u32[]{:S(2)}) collective-permute-start(bf16[2,320,512]{2,1,0:T(8,128)(2,1)S(1)} %get-tuple-element.45), channel_id=1, source_target_pairs={{0,2},{2,0},{4,6},{6,4},{8,10},{10,8},{12,14},{14,12},{16,18},{18,... | collective-permute-start | bytes 1966088 | tf_op jit(solution)/shard_map/ppermute | solution.py:160
  79.5 45.7 %collective-permute-start.14 = (bf16[2,320,512]{2,1,0:T(8,128)(2,1)S(1)}, bf16[2,320,512]{2,1,0:T(8,128)(2,1)S(1)}, u32[]{:S(2)}, u32[]{:S(2)}) collective-permute-start(bf16[2,320,512]{2,1,0:T(8,128)(2,1)S(1)} %get-tuple-element.40), channel_id=1, source_target_pairs={{0,6},{2,4},{4,2},{6,0},{8,14},{10,12},{12,10},{14,8},{16,22},{18,... | collective-permute-start | bytes 1966088 | tf_op jit(solution)/shard_map/ppermute | solution.py:160
  80.2 44.9 %collective-permute-start.13 = (bf16[2,320,512]{2,1,0:T(8,128)(2,1)S(1)}, bf16[2,320,512]{2,1,0:T(8,128)(2,1)S(1)}, u32[]{:S(2)}, u32[]{:S(2)}) collective-permute-start(bf16[2,320,512]{2,1,0:T(8,128)(2,1)S(1)} %get-tuple-element.41), channel_id=1, source_target_pairs={{0,4},{2,6},{4,0},{6,2},{8,12},{10,14},{12,8},{14,10},{16,20},{18,... | collective-permute-start | bytes 1966088 | tf_op jit(solution)/shard_map/ppermute | solution.py:160
  81.9 42.9 %collective-permute-start.12 = (bf16[2,320,512]{2,1,0:T(8,128)(2,1)S(1)}, bf16[2,320,512]{2,1,0:T(8,128)(2,1)S(1)}, u32[]{:S(2)}, u32[]{:S(2)}) collective-permute-start(bf16[2,320,512]{2,1,0:T(8,128)(2,1)S(1)} %get-tuple-element.42), channel_id=1, source_target_pairs={{0,2},{2,0},{4,6},{6,4},{8,10},{10,8},{12,14},{14,12},{16,18},{18,... | collective-permute-start | bytes 1966088 | tf_op jit(solution)/shard_map/ppermute | solution.py:160
  111.8 57.2 %collective-permute-start.15 = (bf16[2,320,512]{2,1,0:T(8,128)(2,1)S(1)}, bf16[2,320,512]{2,1,0:T(8,128)(2,1)}, u32[]{:S(2)}, u32[]{:S(2)}) collective-permute-start(bf16[2,320,512]{2,1,0:T(8,128)(2,1)S(1)} %get-tuple-element.26), channel_id=1, source_target_pairs={{0,2},{2,0},{4,6},{6,4},{8,10},{10,8},{12,14},{14,12},{16,18},{18,... | collective-permute-start | bytes 1966088 | tf_op jit(solution)/shard_map/ppermute | solution.py:160
  117.0 62.4 %collective-permute-start.17 = (bf16[2,320,512]{2,1,0:T(8,128)(2,1)}, bf16[2,320,512]{2,1,0:T(8,128)(2,1)}, u32[]{:S(2)}, u32[]{:S(2)}) collective-permute-start(bf16[2,320,512]{2,1,0:T(8,128)(2,1)} %get-tuple-element.27), channel_id=1, source_target_pairs={{0,6},{2,4},{4,2},{6,0},{8,14},{10,12},{12,10},{14,8},{16,22},{18,... | collective-permute-start | bytes 1966088 | tf_op jit(solution)/shard_map/ppermute | solution.py:160
  124.8 55.9 %collective-permute-start.16 = (bf16[2,320,512]{2,1,0:T(8,128)(2,1)}, bf16[2,320,512]{2,1,0:T(8,128)(2,1)}, u32[]{:S(2)}, u32[]{:S(2)}) collective-permute-start(bf16[2,320,512]{2,1,0:T(8,128)(2,1)} %get-tuple-element.28), channel_id=1, source_target_pairs={{0,4},{2,6},{4,0},{6,2},{8,12},{10,14},{12,8},{14,10},{16,20},{18,... | collective-permute-start | bytes 1966088 | tf_op jit(solution)/shard_map/ppermute | solution.py:160
  154.6 33.2 %collective-permute-start.20 = (bf16[2,320,512]{2,1,0:T(8,128)(2,1)}, bf16[2,320,512]{2,1,0:T(8,128)(2,1)}, u32[]{:S(2)}, u32[]{:S(2)}) collective-permute-start(bf16[2,320,512]{2,1,0:T(8,128)(2,1)} %get-tuple-element.29), channel_id=1, source_target_pairs={{0,2},{2,0},{4,6},{6,4},{8,10},{10,8},{12,14},{14,12},{16,18},{18,... | collective-permute-start | bytes 1966088 | tf_op jit(solution)/shard_map/ppermute | solution.py:160
  159.8 36.0 %collective-permute-start.22 = (bf16[2,320,512]{2,1,0:T(8,128)(2,1)}, bf16[2,320,512]{2,1,0:T(8,128)(2,1)}, u32[]{:S(2)}, u32[]{:S(2)}) collective-permute-start(bf16[2,320,512]{2,1,0:T(8,128)(2,1)} %get-tuple-element.30), channel_id=1, source_target_pairs={{0,6},{2,4},{4,2},{6,0},{8,14},{10,12},{12,10},{14,8},{16,22},{18,... | collective-permute-start | bytes 1966088 | tf_op jit(solution)/shard_map/ppermute | solution.py:160
  169.0 28.0 %collective-permute-start.21 = (bf16[2,320,512]{2,1,0:T(8,128)(2,1)}, bf16[2,320,512]{2,1,0:T(8,128)(2,1)}, u32[]{:S(2)}, u32[]{:S(2)}) collective-permute-start(bf16[2,320,512]{2,1,0:T(8,128)(2,1)} %get-tuple-element.31), channel_id=1, source_target_pairs={{0,4},{2,6},{4,0},{6,2},{8,12},{10,14},{12,8},{14,10},{16,20},{18,... | collective-permute-start | bytes 1966088 | tf_op jit(solution)/shard_map/ppermute | solution.py:160
  182.0 19.4 %copy-start = (f32[2,320,512]{2,1,0:T(8,128)}, f32[2,320,512]{2,1,0:T(8,128)S(1)}, u32[]{:S(2)}) copy-start(f32[2,320,512]{2,1,0:T(8,128)S(1)} %convert_element_type.89) | copy-start | bytes 3932164
  183.7 39.7 %collective-permute-start.18 = (bf16[320,512]{1,0:T(8,128)(2,1)S(1)}, bf16[320,512]{1,0:T(8,128)(2,1)}, u32[]{:S(2)}, u32[]{:S(2)}) collective-permute-start(bf16[320,512]{1,0:T(8,128)(2,1)S(1)} %get-tuple-element.22), channel_id=1, source_target_pairs={{8,0},{10,2},{12,4},{14,6},{16,8},{18,10},{20,12},{22,14},{24,16},... | collective-permute-start | bytes 983048 | tf_op jit(solution)/shard_map/ppermute | solution.py:154
  185.7 37.7 %collective-permute-start.19 = (bf16[320,512]{1,0:T(8,128)(2,1)S(1)}, bf16[320,512]{1,0:T(8,128)(2,1)}, u32[]{:S(2)}, u32[]{:S(2)}) collective-permute-start(bf16[320,512]{1,0:T(8,128)(2,1)S(1)} %get-tuple-element.23), channel_id=1, source_target_pairs={{16,0},{18,2},{20,4},{22,6},{24,8},{26,10},{28,12},{30,14},{17,1},... | collective-permute-start | bytes 983048 | tf_op jit(solution)/shard_map/ppermute | solution.py:154
  189.0 12.4 %copy-start.1 = (f32[2,320,512]{2,1,0:T(8,128)}, f32[2,320,512]{2,1,0:T(8,128)S(1)}, u32[]{:S(2)}) copy-start(f32[2,320,512]{2,1,0:T(8,128)S(1)} %convert_element_type.98) | copy-start | bytes 3932164
  197.0 4.3 %copy-start.3 = (f32[2,320,512]{2,1,0:T(8,128)}, f32[2,320,512]{2,1,0:T(8,128)S(1)}, u32[]{:S(2)}) copy-start(f32[2,320,512]{2,1,0:T(8,128)S(1)} %convert_element_type.100) | copy-start | bytes 3932164
  201.4 23.9 %collective-permute-start.23 = (bf16[320,512]{1,0:T(8,128)(2,1)}, bf16[320,512]{1,0:T(8,128)(2,1)}, u32[]{:S(2)}, u32[]{:S(2)}) collective-permute-start(bf16[320,512]{1,0:T(8,128)(2,1)} %get-tuple-element.24), channel_id=1, source_target_pairs={{8,0},{10,2},{12,4},{14,6},{16,8},{18,10},{20,12},{22,14},{24,16},... | collective-permute-start | bytes 983048 | tf_op jit(solution)/shard_map/ppermute | solution.py:154
  203.4 21.9 %collective-permute-start.24 = (bf16[320,512]{1,0:T(8,128)(2,1)}, bf16[320,512]{1,0:T(8,128)(2,1)}, u32[]{:S(2)}, u32[]{:S(2)}) collective-permute-start(bf16[320,512]{1,0:T(8,128)(2,1)} %get-tuple-element.25), channel_id=1, source_target_pairs={{16,0},{18,2},{20,4},{22,6},{24,8},{26,10},{28,12},{30,14},{17,1},... | collective-permute-start | bytes 983048 | tf_op jit(solution)/shard_map/ppermute | solution.py:154
  231.7 6.6 %copy-start.7 = (bf16[320,512]{1,0:T(8,128)(2,1)}, bf16[320,512]{1,0:T(8,128)(2,1)S(1)}, u32[]{:S(2)}) copy-start(bf16[320,512]{1,0:T(8,128)(2,1)S(1)} %get-tuple-element.55) | copy-start | bytes 983044
  231.7 6.6 %copy-start.6 = (bf16[320,512]{1,0:T(8,128)(2,1)}, bf16[320,512]{1,0:T(8,128)(2,1)S(1)}, u32[]{:S(2)}) copy-start(bf16[320,512]{1,0:T(8,128)(2,1)S(1)} %get-tuple-element.54) | copy-start | bytes 983044
  244.1 7.2 %collective-permute-start.25 = (bf16[320,2560]{1,0:T(8,128)(2,1)}, bf16[320,2560]{1,0:T(8,128)(2,1)}, u32[]{:S(2)}, u32[]{:S(2)}) collective-permute-start(bf16[320,2560]{1,0:T(8,128)(2,1)} %constant_dynamic-slice_fusion), channel_id=1, source_target_pairs={{0,1},{1,0},{2,3},{3,2},{4,5},{5,4},{6,7},{7,6},{8,9},{9,8},{10,11... | collective-permute-start | bytes 4915208 | tf_op jit(solution)/shard_map/ppermute | solution.py:273
  (6 other events, 13.7 us)
